TPU v7x, 32 devices: a whole 2x2x4 slice. The times are simulated.
32 devices in a mesh: rows: 8 (over z, y), feat: 4 (over x, core).
Axes of the slice: x: 2, y: 2, z: 4, core: 2. Of those that a mesh axis runs over, the one named last changes fastest.
Arguments:
- bin_codes: int32 [32768, 2048], P('rows', 'feat'), may hold values from 0 to 255
- gradient: bfloat16 [32768], P('rows'), may hold values from -6 to 6
- hessian: bfloat16 [32768], P('rows'), may hold values from 0.049804688 to 1
- leaf_of_block: int32 [256], P('rows'), may hold values from 0 to 1
- block_rows: int32 [256], P('rows'), may hold values from 32 to 128, as said below
Outputs:
- split_gain: float32 [2, 2048, 256], P(None, ('feat', 'rows'))
- best_gain: float32 [2], replicated
Inputs may be any that keep to these rules, and one draw needn't show every extreme that they name: `block_rows`: the live rows are the first ones of their block; some block is full in every draw.
All inputs are finite; a program needn't handle non-finite values.
Results may differ from a plain program's by a relative error of at most 0.0003.
Values sent between devices are 32-bit elements; how exact they have to be, the bound alone decides.
No kernel may reach another device: no remote copies, remote signals or barrier semaphores. Data moves between devices by JAX's collectives and lax.ppermute only.
A program may use at most 64 MiB of HBM per device.

v0:
```python
import functools

import jax
import jax.numpy as jnp
from jax import lax
from jax.experimental import pallas as pl
from jax.experimental.pallas import tpu as pltpu
from jax.sharding import PartitionSpec as P

BINS = 256
LEAVES = 2
BLOCK = 128
MIN_CHILD = 20
RIDGE = 1.0

STATS = 3
HIGH = 8
LOW = 32
FOLD = 8
PAIR = 2 * FOLD
WIDTH = LOW * FOLD
ROWS = HIGH * FOLD
DEPTH = STATS * ROWS
TILE = 256
BIG = 3 * TILE
SPAN = 512
WAYS = 4
PLAN = (([(1,1),(2,1)], []), ([(3,1),(0,0)], [0]), ([(2,0),(1,0)], [2,0]), ([(3,0)], [1,2]), ([], [3,1,3]))
SUMS = (2, LEAVES, STATS, FOLD, WIDTH)

BF = jnp.bfloat16
F32 = jnp.float32
VMEM_BYTES = 24 << 20
MOST_VMEM = 54 << 20


def nt(a, b):
    return lax.dot_general(a, b, (((1,), (1,)), ((), ())), preferred_element_type=F32)


def in_vmem(x):
    return pltpu.with_memory_space_constraint(x, pltpu.VMEM)


def live_up(count):
    return (count + 15) // 16 * 16


def tiles_of(total):
    return (total + TILE - 1) // TILE


def pack_kernel(
    blocks, first_rows,
    pos_ref, leaf_ref, rows_ref, codes_ref, grad_ref, hess_ref,
    table_ref, weight_ref, sums_ref, info_ref,
    arrived, held, rows_held, pair_held, total, offset, ends, in_sem, pair_sem,
):
    steps = blocks * BLOCK // SPAN
    per_step = SPAN // BLOCK
    feats = held.shape[1]

    def fetch(i):
        return pltpu.make_async_copy(
            codes_ref.at[pl.ds(pl.multiple_of(i * SPAN, SPAN), SPAN), :], arrived.at[i], in_sem.at[i]
        )

    pairs = [
        pltpu.make_async_copy(ref, pair_held.at[i], pair_sem.at[i]) for i, ref in enumerate((grad_ref, hess_ref))
    ]
    for copy in pairs:
        copy.start()
    for i in range(steps):
        fetch(i).start()

    def count(k, room):
        size, leaf = live_up(rows_ref[k]), leaf_ref[k]
        return room[0] + size * (1 - leaf), room[1] + size * leaf

    first, second = lax.fori_loop(0, blocks, count, (0, 0), unroll=4)
    start = tiles_of(first) * TILE + BLOCK

    def place(k, room):
        offset[k] = jnp.where(leaf_ref[k] == 0, room[0], room[1])
        room = count(k, room)
        ends[0, k], ends[1, k] = room
        return room

    lax.fori_loop(0, blocks, place, (0, start), unroll=4)
    info_ref[0] = tiles_of(first)
    info_ref[1] = tiles_of(second)
    info_ref[2] = start
    info_ref[3] = pos_ref[0]

    rows_held[...] = jnp.zeros_like(rows_held)
    for copy in pairs:
        copy.wait()
    grads, hessians = pair_held[0].astype(F32), pair_held[1].astype(F32)
    lane = lax.broadcasted_iota(jnp.int32, (8, BLOCK), 1)
    row = lax.broadcasted_iota(jnp.int32, (8, BLOCK), 0)
    rolled = []
    for k in range(blocks):
        grad = jnp.broadcast_to(grads[k : k + 1], (8, BLOCK))
        hess = jnp.broadcast_to(hessians[k : k + 1], (8, BLOCK))
        value = jnp.where(row == 0, grad, jnp.where(row == 1, hess, jnp.where(row == 2, 1.0, 0.0)))
        value = jnp.where(lane < rows_ref[k], value, 0.0)
        rolled.append(pltpu.roll(value, lax.rem(offset[k], BLOCK), 1))
    for k in range(blocks):
        at = offset[k]
        shift = lax.rem(at, BLOCK)
        tile = pl.multiple_of(at - shift, BLOCK)
        here = rows_held[:, pl.ds(tile, BLOCK)]
        rows_held[:, pl.ds(tile, BLOCK)] = jnp.where(lane < shift, here, rolled[k])
        after = pl.ds(pl.multiple_of(tile + BLOCK, BLOCK), BLOCK)
        rows_held[:, after] = jnp.where(lane < shift, rolled[k], 0.0)

    size = 256
    eye = (
        lax.broadcasted_iota(jnp.int32, (size, size), 0) == lax.broadcasted_iota(jnp.int32, (size, size), 1)
    ).astype(F32).astype(BF)

    def turn(base, tiles, done):
        @pl.loop(done, tiles)
        def _(j):
            at = pl.multiple_of(base + j * TILE, BLOCK)
            for f in range(0, feats, size):
                table_ref[f : f + size, pl.ds(at, TILE)] = nt(eye, held[pl.ds(at, TILE), f : f + size]).astype(BF)
            for s in range(STATS):
                weight_ref[s, :, pl.ds(at, TILE)] = jnp.broadcast_to(
                    rows_held[s : s + 1, pl.ds(at, TILE)], (16, TILE)
                ).astype(BF)

        return jnp.maximum(done, tiles)

    def step(i, done):
        fetch(i).wait()
        for j in range(per_step):
            at = pl.multiple_of(offset[i * per_step + j], 16)
            held[pl.ds(at, BLOCK), :] = arrived[i, j * BLOCK : (j + 1) * BLOCK, :].astype(F32).astype(BF)
        last = (i + 1) * per_step - 1
        return (
            turn(0, ends[0, last] // TILE, done[0]),
            turn(start, (ends[1, last] - start) // TILE, done[1]),
        )

    done = lax.fori_loop(0, steps, step, (0, 0))
    turn(0, tiles_of(first), done[0])
    turn(start, tiles_of(second), done[1])
    histogram_into(first_rows(info_ref), info_ref, table_ref, weight_ref, [sums_ref], total)


def pack(pos, leaf_of_block, block_rows, codes, gradient, hessian, room, first_rows):
    row_total, feat_local = codes.shape
    blocks = row_total // BLOCK
    steps = row_total // SPAN
    whole, anywhere = pl.BlockSpec(memory_space=pltpu.VMEM), pl.BlockSpec(memory_space=pl.ANY)
    return pl.pallas_call(
        functools.partial(pack_kernel, blocks, first_rows),
        grid_spec=pltpu.PrefetchScalarGridSpec(
            num_scalar_prefetch=3,
            grid=(1,),
            in_specs=[anywhere] * 3,
            out_specs=[whole, whole, whole, pl.BlockSpec(memory_space=pltpu.SMEM)],
            scratch_shapes=[
                pltpu.VMEM((steps, SPAN, feat_local), jnp.int32),
                pltpu.VMEM((room, feat_local), BF),
                pltpu.VMEM((8, room), F32),
                pltpu.VMEM((2, blocks, BLOCK), BF),
                pltpu.VMEM((2 * WAYS, DEPTH, WIDTH), F32),
                pltpu.SMEM((blocks,), jnp.int32),
                pltpu.SMEM((2, blocks), jnp.int32),
                pltpu.SemaphoreType.DMA((steps,)),
                pltpu.SemaphoreType.DMA((2,)),
            ],
        ),
        out_shape=[
            pltpu.VMEM((feat_local, room), BF),
            pltpu.VMEM((STATS, 16, room), BF),
            pltpu.VMEM((WAYS,) + SUMS, F32),
            jax.ShapeDtypeStruct((8,), jnp.int32),
        ],
        compiler_params=pltpu.CompilerParams(vmem_limit_bytes=MOST_VMEM),
        cost_estimate=pl.CostEstimate(flops=4 << 30, bytes_accessed=16 << 20, transcendentals=0),
    )(pos, leaf_of_block, block_rows, codes, gradient.reshape(blocks, BLOCK), hessian.reshape(blocks, BLOCK))


def histogram_kernel(first_rows, info_ref, table_ref, weight_ref, *refs):
    histogram_into(first_rows(info_ref), info_ref, table_ref, weight_ref, refs[:-1], refs[-1])


def histogram_into(starts, info_ref, table_ref, weight_ref, outs, total):
    lane = lax.broadcasted_iota(jnp.int32, (FOLD, WIDTH), 1)
    skew = (lax.broadcasted_iota(jnp.int32, (FOLD, WIDTH), 0) - lane) & (FOLD - 1)

    def product(at, size, fresh):
        half = (lax.broadcasted_iota(jnp.int32, (16, size), 0) >> 3).astype(F32).astype(BF)
        nth = (lax.broadcasted_iota(jnp.int32, (size, 128), 1) >> 3).astype(F32).astype(BF)
        one, zero = jnp.ones((size, 128), BF), jnp.zeros((size, 128), BF)
        none = jnp.zeros((16, size), BF)
        weights = [weight_ref[s, :, pl.ds(at, size)] for s in range(STATS)]
        for way in range(len(starts)):
            both = table_ref[pl.ds(starts[way], PAIR), pl.ds(at, size)].astype(F32)
            for i in range(2):
                code = both[i * FOLD : (i + 1) * FOLD]
                high = jnp.floor(code * (1.0 / LOW))
                low = code - high * LOW
                high = jnp.concatenate([high] * 2, 0).astype(BF) - half
                masks = [high == BF(q) for q in range(0, HIGH, 2)]
                terms = jnp.concatenate([jnp.where(m, w, none) for w in weights for m in masks], 0)
                low = jnp.concatenate([jnp.concatenate([low] * 2, 0).astype(BF)] * 8, 0).T - nth
                picks = jnp.concatenate([jnp.where(low == BF(q), one, zero) for q in (0, 16)], 1)
                sums = lax.dot_general(terms, picks, (((1,), (0,)), ((), ())), preferred_element_type=F32)
                total[2 * way + i] = jnp.where(fresh, 0.0, total[2 * way + i]) + sums

    for leaf in range(LEAVES):
        start = info_ref[2] if leaf else 0
        tiles = info_ref[leaf]
        big = tiles // 3
        rest = tiles - 3 * big

        @pl.when(tiles == 0)
        def _():
            total[...] = jnp.zeros_like(total)

        @pl.loop(0, big)
        def _(k):
            product(pl.multiple_of(start + k * BIG, BLOCK), BIG, k == 0)

        at = start + big * BIG

        @pl.when(rest == 2)
        def _():
            product(pl.multiple_of(at, BLOCK), 2 * TILE, tiles == 2)

        @pl.when(rest == 1)
        def _():
            product(pl.multiple_of(at, BLOCK), TILE, tiles == 1)

        for way in range(len(starts)):
            for i in range(2):
                for s in range(STATS):
                    base = s * ROWS
                    value = total[2 * way + i, base : base + FOLD]
                    for h in range(1, HIGH):
                        piece = total[2 * way + i, base + h * FOLD : base + (h + 1) * FOLD]
                        value = jnp.where(skew == h, pltpu.roll(piece, h, 0), value)
                    outs[way // WAYS][way % WAYS, i, leaf, s] = value


def rows_of(per_owner, jobs):
    def first_rows(info_ref):
        return [
            pl.multiple_of((info_ref[3] ^ way) * per_owner + pair * PAIR, PAIR) for pair, ways in jobs for way in ways
        ]

    return first_rows


def histogram(packed, owners, jobs):
    table, weight, info = packed
    first_rows = rows_of(table.shape[0] // owners, jobs)
    whole = pl.BlockSpec(memory_space=pltpu.VMEM)
    return pl.pallas_call(
        functools.partial(histogram_kernel, first_rows),
        grid_spec=pltpu.PrefetchScalarGridSpec(
            num_scalar_prefetch=1,
            grid=(1,),
            in_specs=[whole, whole],
            out_specs=[whole] * len(jobs),
            scratch_shapes=[pltpu.VMEM((2 * WAYS * len(jobs), DEPTH, WIDTH), F32)],
        ),
        out_shape=[pltpu.VMEM((WAYS,) + SUMS, F32)] * len(jobs),
        compiler_params=pltpu.CompilerParams(vmem_limit_bytes=VMEM_BYTES),
        cost_estimate=pl.CostEstimate(flops=(6 << 30) * len(jobs), bytes_accessed=4 << 20, transcendentals=0),
    )(info, in_vmem(table), in_vmem(weight))


def pick(x, chooser):
    total = 0.0
    for _ in range(3):
        part = x.astype(BF)
        total = total + lax.dot_general(part, chooser, (((1,), (0,)), ((), ())), preferred_element_type=F32)
        x = x - part.astype(F32)
    return total


def gain_kernel(chunks, *refs):
    own, others, gain_ref, top_ref = refs[:chunks], refs[chunks : 2 * chunks], refs[-2], refs[-1]
    before = refs[2 * chunks + 1] if len(refs) > 2 * chunks + 2 else None
    lane = lax.broadcasted_iota(jnp.int32, (FOLD, WIDTH), 1)
    row = lax.broadcasted_iota(jnp.int32, (FOLD, WIDTH), 0)
    rows = lax.broadcasted_iota(jnp.int32, (WIDTH, WIDTH), 0)
    cols = lax.broadcasted_iota(jnp.int32, (WIDTH, WIDTH), 1)

    def chooser(mask):
        return jnp.where(mask, 1.0, 0.0).astype(BF)

    same = (rows & 7) == (cols & 7)
    upto = chooser(same & ((rows >> 3) <= (cols >> 3)))
    same = chooser(same)
    order = chooser(((rows & 7) == (cols >> 5)) & ((rows >> 3) == (cols & 31)))
    apart = (row - (lane >> 5)) & 7
    tops = [jnp.full((FOLD, WIDTH), -jnp.inf, F32)] * LEAVES
    for c in range(chunks):
        pieces = []
        for i in range(2):
            for leaf in range(LEAVES):
                for s in range(STATS):
                    x = own[c][0, i, leaf, s] + others[c][0, i, leaf, s]
                    for bit in (1, 2, 4):
                        x = jnp.where((lane & bit) != 0, pltpu.roll(x, FOLD - bit, 0), x)
                    pieces.append(x)
        stacked = jnp.concatenate(pieces, 0)
        inner = pick(stacked, upto)
        whole = pick(stacked, same)
        gains = []
        for i in range(2):
            for leaf in range(LEAVES):
                left, total = [], []
                for s in range(STATS):
                    at = ((i * LEAVES + leaf) * STATS + s) * FOLD
                    run = whole[at : at + FOLD]
                    for step in (1, 2, 4):
                        run = run + jnp.where(row >= step, pltpu.roll(run, step, 0), 0.0)
                    lower = jnp.where(row >= 1, pltpu.roll(run, 1, 0), 0.0)
                    left.append(inner[at : at + FOLD] + lower)
                    total.append(jnp.broadcast_to(run[FOLD - 1 : FOLD], (FOLD, WIDTH)))
                right = [t - a for t, a in zip(total, left)]
                raw = 0.5 * (
                    left[0] * left[0] / (left[1] + RIDGE)
                    + right[0] * right[0] / (right[1] + RIDGE)
                    - total[0] * total[0] / (total[1] + RIDGE)
                )
                value = jnp.where((left[2] >= MIN_CHILD) & (right[2] >= MIN_CHILD), raw, 0.0)
                gains.append(value)
                tops[leaf] = jnp.maximum(tops[leaf], value)
        z = pick(jnp.concatenate(gains, 0), order)
        for i in range(2):
            for leaf in range(LEAVES):
                at = (i * LEAVES + leaf) * FOLD
                piece = z[at : at + FOLD]
                out = jnp.where(apart == 0, piece, 0.0)
                for d in range(1, FOLD):
                    part = jnp.where(apart == d, piece, 0.0)
                    out = out + pltpu.roll(pltpu.roll(part, FOLD - d, 0), LOW * d, 1)
                gain_ref[leaf, c * PAIR + i * FOLD : c * PAIR + (i + 1) * FOLD, :] = out
    tops = [jnp.max(top, axis=(0, 1), keepdims=True) for top in tops]
    at = lax.broadcasted_iota(jnp.int32, top_ref.shape, 1)
    top = jnp.where(at == 0, tops[0], tops[1])
    top_ref[...] = top if before is None else jnp.maximum(top, before[...])


def gain(own, others, first, features, devices, done):
    count = len(own)
    top = (devices, 128)
    rows = count * PAIR
    return pl.pallas_call(
        functools.partial(gain_kernel, count),
        grid=(1,),
        in_specs=[pl.BlockSpec((1,) + SUMS, lambda i: (0,) * 6)] * (2 * count)
        + ([pl.BlockSpec(memory_space=pl.ANY), pl.BlockSpec(top, lambda i: (0, 0))] if done else []),
        out_specs=[
            pl.BlockSpec((LEAVES, rows, BINS), lambda i: (0, first // count, 0)),
            pl.BlockSpec(top, lambda i: (0, 0)),
        ],
        out_shape=[jax.ShapeDtypeStruct((LEAVES, features, BINS), F32), jax.ShapeDtypeStruct(top, F32)],
        input_output_aliases={2 * count: 0, 2 * count + 1: 1} if done else {},
        compiler_params=pltpu.CompilerParams(vmem_limit_bytes=VMEM_BYTES),
        cost_estimate=pl.CostEstimate(flops=1 << 30, bytes_accessed=1 << 20, transcendentals=0),
    )(*own, *others, *done)


def in_halves(ways, bits):
    if not bits:
        return ways
    return in_halves([w for w in ways if not w & bits[0]], bits[1:]) + in_halves(
        [w for w in ways if w & bits[0]], bits[1:]
    )


def joined(arrays):
    return arrays[0] if len(arrays) == 1 else jnp.concatenate(arrays, 0)


def in_turn(packed, done):
    return (*packed[:2], lax.optimization_barrier((packed[2], *done))[0])


def local(owners, devices, bin_codes, gradient, hessian, leaf_of_block, block_rows):
    row_total, feat_local = bin_codes.shape
    pos = lax.axis_index("rows").astype(jnp.int32)[None]
    room = -(-(row_total + 2 * TILE + BLOCK) // SPAN) * SPAN
    pairs = feat_local // owners // PAIR
    bits = [1 << b for b in range(1, owners.bit_length() - 1)]
    kept = in_halves([w for w in range(owners) if not w & 1], bits)
    parts = [kept[i : i + WAYS] for i in range(0, len(kept), WAYS)]

    def swap(x, bit):
        return lax.ppermute(x, "rows", [(i, i ^ bit) for i in range(owners)])

    def ways_of(side, part):
        return [w ^ side for w in part]

    first_rows = rows_of(feat_local // owners, [(0, ways_of(1, parts[0]))])
    *packed, first, info = pack(
        pos, leaf_of_block, block_rows, bin_codes, gradient, hessian, room, first_rows
    )
    packed = (*packed, info)
    keep, other, left = {}, {0: [swap(first, 1)]}, {pair: bits for pair in range(pairs)}
    plan = PLAN
    if pairs != 4:
        plan = [([(pair, side)], []) for pair in range(pairs) for side in (1, 0)]
        plan += [([], [pair for pair in range(pairs) for _ in bits])]
    for jobs, exchanges in plan:
        for n, part in enumerate(parts):
            todo = [job for job in jobs if n or job != (0, 1)]
            if not todo:
                continue
            sums = histogram(packed, owners, [(pair, ways_of(side, part)) for pair, side in todo])
            for (pair, side), x in zip(todo, sums):
                (other if side else keep).setdefault(pair, []).append(swap(x, 1) if side else x)
            packed = in_turn(packed, sums)
        moved = []
        for pair in exchanges:
            if isinstance(keep[pair], list):
                keep[pair], other[pair] = joined(keep[pair]), joined(other[pair])
            mine, theirs, (bit, *left[pair]) = keep[pair], other[pair], left[pair]
            half = mine.shape[0] // 2
            on = mine[half:] + theirs[half:]
            moved.append(on)
            keep[pair], other[pair] = mine[:half] + theirs[:half], swap(on, bit)
        packed = in_turn(packed, moved)
    done = ()
    for group in (range(pairs - 1), range(pairs - 1, pairs)):
        if group:
            done = gain(
                [keep[p] for p in group], [other[p] for p in group], group[0], feat_local // owners, devices, done
            )
    split_gain, best = done
    best = lax.all_to_all(best, ("rows", "feat"), 0, 0, tiled=True)
    return split_gain, jnp.max(best, axis=0)[:LEAVES]


def solution(mesh):
    return jax.shard_map(
        functools.partial(local, mesh.shape["rows"], mesh.size),
        mesh=mesh,
        in_specs=(P("rows", "feat"), P("rows"), P("rows"), P("rows"), P("rows")),
        out_specs=(P(None, ("feat", "rows"), None), P()),
        check_vma=False,
    )
```

profile of v0, /device:TPU:0, one launch (start us, length us, event | category | flops | bytes accessed | tf_op | source)
XLA Modules:
  0.0 84.7 jit_solution(6779625342555981691)
XLA Ops:
  0.6 11.2 %shard_map.68 = (bf16[512,5120]{1,0:T(8,128)(2,1)S(1)}, bf16[3,16,5120]{2,1,0:T(8,128)(2,1)S(1)}, f32[4,2,2,3,8,256]{5,4,3,2,1,0:T(8,128)S(1)}, s32[8]{0:T(128)}) custom-call(s32[1]{0:T(128)} %bitcast.pos_ref, s32[32]{0:T(128)} %leaf_ref.1, s32[32]{0:T(128)} %rows_ref.1, s32[4096,512]{1,0:T(8,128)} %codes_ref.1, bf16[32,128]{1,0:T(8,128)(2,1)} %bitcast.9, ...), custom_call_target="tpu_custom_call" | custom-call | flops 4294967296 | bytes 16777216 | tf_op jit(solution)/shard_map/pallas_call | solution.py:157
  11.8 3.0 %collective-permute-start = (f32[4,2,2,3,8,256]{5,4,3,2,1,0:T(8,128)S(1)}, f32[4,2,2,3,8,256]{5,4,3,2,1,0:T(8,128)S(1)}, u32[]{:S(2)}, u32[]{:S(2)}) collective-permute-start(f32[4,2,2,3,8,256]{5,4,3,2,1,0:T(8,128)S(1)} %get-tuple-element.30), channel_id=1, source_target_pairs={{0,4},{4,0},{8,12},{12,8},{16,20},{20,16},{24,28},{28,24},{1,5},{5... | collective-permute-start | bytes 1179656 | tf_op jit(solution)/shard_map/ppermute | solution.py:399
  14.9 0.0 copy-start
  14.9 0.7 copy-done
  15.5 6.7 %shard_map.69 = (f32[4,2,2,3,8,256]{5,4,3,2,1,0:T(8,128)S(1)}, f32[4,2,2,3,8,256]{5,4,3,2,1,0:T(8,128)S(1)}) custom-call(s32[8]{0:T(128)S(1)} %copy-done, bf16[512,5120]{1,0:T(8,128)(2,1)S(1)} %get-tuple-element.22.table_ref, bf16[3,16,5120]{2,1,0:T(8,128)(2,1)S(1)} %get-tuple-element.23.weight_ref), custom_call_target="tpu_custom_call" | custom-call | flops 12884901888 | bytes 4194304 | tf_op jit(solution)/shard_map/pallas_call | solution.py:263
  22.3 0.1 collective-permute-start.6
  22.4 2.0 %collective-permute-start.1 = (f32[4,2,2,3,8,256]{5,4,3,2,1,0:T(8,128)S(1)}, f32[4,2,2,3,8,256]{5,4,3,2,1,0:T(8,128)S(1)}, u32[]{:S(2)}, u32[]{:S(2)}) collective-permute-start(f32[4,2,2,3,8,256]{5,4,3,2,1,0:T(8,128)S(1)} %get-tuple-element.25), channel_id=1, source_target_pairs={{0,4},{4,0},{8,12},{12,8},{16,20},{20,16},{24,28},{28,24},{1,5},{5... | collective-permute-start | bytes 1179656 | tf_op jit(solution)/shard_map/ppermute | solution.py:399
  24.4 6.5 %shard_map.70 = (f32[4,2,2,3,8,256]{5,4,3,2,1,0:T(8,128)S(1)}, f32[4,2,2,3,8,256]{5,4,3,2,1,0:T(8,128)S(1)}) custom-call(s32[8]{0:T(128)S(1)} %copy-done, bf16[512,5120]{1,0:T(8,128)(2,1)S(1)} %get-tuple-element.22.table_ref, bf16[3,16,5120]{2,1,0:T(8,128)(2,1)S(1)} %get-tuple-element.23.weight_ref), custom_call_target="tpu_custom_call" | custom-call | flops 12884901888 | bytes 4194304 | tf_op jit(solution)/shard_map/pallas_call | solution.py:263
  30.9 0.1 collective-permute-start.3
  31.1 0.0 collective-permute-done
  31.1 0.1 slice_add_fusion.5
  31.1 3.9 %collective-permute-start.2 = (f32[2,2,2,3,8,256]{5,4,3,2,1,0:T(8,128)S(1)}, f32[2,2,2,3,8,256]{5,4,3,2,1,0:T(8,128)S(1)}, u32[]{:S(2)}, u32[]{:S(2)}) collective-permute-start(f32[2,2,2,3,8,256]{5,4,3,2,1,0:T(8,128)S(1)} %get-tuple-element.47), channel_id=1, source_target_pairs={{0,8},{4,12},{8,0},{12,4},{16,24},{20,28},{24,16},{28,20},{1,9},{5... | collective-permute-start | bytes 589832 | tf_op jit(solution)/shard_map/ppermute | solution.py:399
  35.0 6.8 %shard_map.71 = (f32[4,2,2,3,8,256]{5,4,3,2,1,0:T(8,128)S(1)}, f32[4,2,2,3,8,256]{5,4,3,2,1,0:T(8,128)S(1)}) custom-call(s32[8]{0:T(128)S(1)} %copy-done, bf16[512,5120]{1,0:T(8,128)(2,1)S(1)} %get-tuple-element.22.table_ref, bf16[3,16,5120]{2,1,0:T(8,128)(2,1)S(1)} %get-tuple-element.23.weight_ref), custom_call_target="tpu_custom_call" | custom-call | flops 12884901888 | bytes 4194304 | tf_op jit(solution)/shard_map/pallas_call | solution.py:263
  41.8 0.0 collective-permute-done.6
  41.8 0.1 slice_add_fusion.2
  41.9 0.5 collective-permute-start.7
  42.4 0.4 collective-permute-done.1
  42.8 0.1 slice_add_fusion
  42.9 2.9 %collective-permute-start.8 = (f32[2,2,2,3,8,256]{5,4,3,2,1,0:T(8,128)S(1)}, f32[2,2,2,3,8,256]{5,4,3,2,1,0:T(8,128)S(1)}, u32[]{:S(2)}, u32[]{:S(2)}) collective-permute-start(f32[2,2,2,3,8,256]{5,4,3,2,1,0:T(8,128)S(1)} %get-tuple-element.41), channel_id=1, source_target_pairs={{0,8},{4,12},{8,0},{12,4},{16,24},{20,28},{24,16},{28,20},{1,9},{5... | collective-permute-start | bytes 589832 | tf_op jit(solution)/shard_map/ppermute | solution.py:399
  45.7 0.0 collective-permute-done.2
  45.8 3.5 %collective-permute-start.9 = (f32[1,2,2,3,8,256]{5,4,3,2,1,0:T(8,128)S(1)}, f32[1,2,2,3,8,256]{5,4,3,2,1,0:T(8,128)S(1)}, u32[]{:S(2)}, u32[]{:S(2)}) collective-permute-start(f32[1,2,2,3,8,256]{5,4,3,2,1,0:T(8,128)S(1)} %get-tuple-element.53), channel_id=1, source_target_pairs={{0,16},{4,20},{8,24},{12,28},{16,0},{20,4},{24,8},{28,12},{1,17},{... | collective-permute-start | bytes 294920 | tf_op jit(solution)/shard_map/ppermute | solution.py:399
  49.2 4.0 %shard_map.72 = f32[4,2,2,3,8,256]{5,4,3,2,1,0:T(8,128)S(1)} custom-call(s32[8]{0:T(128)S(1)} %copy-done, bf16[512,5120]{1,0:T(8,128)(2,1)S(1)} %get-tuple-element.22.table_ref, bf16[3,16,5120]{2,1,0:T(8,128)(2,1)S(1)} %get-tuple-element.23.weight_ref), custom_call_target="tpu_custom_call" | custom-call | flops 6442450944 | bytes 4194304 | tf_op jit(solution)/shard_map/pallas_call | solution.py:263
  53.3 0.0 collective-permute-done.3
  53.3 0.1 slice_add_fusion.4
  53.3 1.1 %collective-permute-start.4 = (f32[2,2,2,3,8,256]{5,4,3,2,1,0:T(8,128)S(1)}, f32[2,2,2,3,8,256]{5,4,3,2,1,0:T(8,128)S(1)}, u32[]{:S(2)}, u32[]{:S(2)}) collective-permute-start(f32[2,2,2,3,8,256]{5,4,3,2,1,0:T(8,128)S(1)} %get-tuple-element.45), channel_id=1, source_target_pairs={{0,8},{4,12},{8,0},{12,4},{16,24},{20,28},{24,16},{28,20},{1,9},{5... | collective-permute-start | bytes 589832 | tf_op jit(solution)/shard_map/ppermute | solution.py:399
  54.5 0.0 collective-permute-done.7
  54.5 0.8 collective-permute-start.10
  55.4 0.0 collective-permute-done.8
  55.4 3.7 %collective-permute-start.11 = (f32[1,2,2,3,8,256]{5,4,3,2,1,0:T(8,128)S(1)}, f32[1,2,2,3,8,256]{5,4,3,2,1,0:T(8,128)S(1)}, u32[]{:S(2)}, u32[]{:S(2)}) collective-permute-start(f32[1,2,2,3,8,256]{5,4,3,2,1,0:T(8,128)S(1)} %get-tuple-element.48), channel_id=1, source_target_pairs={{0,16},{4,20},{8,24},{12,28},{16,0},{20,4},{24,8},{28,12},{1,17},{... | collective-permute-start | bytes 294920 | tf_op jit(solution)/shard_map/ppermute | solution.py:399
  59.1 1.7 %collective-permute-done.4 = f32[2,2,2,3,8,256]{5,4,3,2,1,0:T(8,128)S(1)} collective-permute-done((f32[2,2,2,3,8,256]{5,4,3,2,1,0:T(8,128)S(1)}, f32[2,2,2,3,8,256]{5,4,3,2,1,0:T(8,128)S(1)}, u32[]{:S(2)}, u32[]{:S(2)}) %collective-permute-start.4) | collective-permute-done | bytes 196640 | tf_op jit(solution)/shard_map/ppermute | solution.py:399
  60.8 4.6 %collective-permute-start.5 = (f32[1,2,2,3,8,256]{5,4,3,2,1,0:T(8,128)S(1)}, f32[1,2,2,3,8,256]{5,4,3,2,1,0:T(8,128)S(1)}, u32[]{:S(2)}, u32[]{:S(2)}) collective-permute-start(f32[1,2,2,3,8,256]{5,4,3,2,1,0:T(8,128)S(1)} %get-tuple-element.54), channel_id=1, source_target_pairs={{0,16},{4,20},{8,24},{12,28},{16,0},{20,4},{24,8},{28,12},{1,17},{... | collective-permute-start | bytes 294920 | tf_op jit(solution)/shard_map/ppermute | solution.py:399
  65.4 0.0 collective-permute-done.9.refs_3_
  65.4 0.0 collective-permute-done.10.refs_4_
  65.5 3.8 %collective-permute-done.11.refs_5_ = f32[1,2,2,3,8,256]{5,4,3,2,1,0:T(8,128)S(1)} collective-permute-done((f32[1,2,2,3,8,256]{5,4,3,2,1,0:T(8,128)S(1)}, f32[1,2,2,3,8,256]{5,4,3,2,1,0:T(8,128)S(1)}, u32[]{:S(2)}, u32[]{:S(2)}) %collective-permute-start.11) | collective-permute-done | bytes 98336 | tf_op jit(solution)/shard_map/ppermute | solution.py:399
  69.3 2.0 %shard_map.73 = (f32[2,64,256]{2,1,0:T(8,128)}, f32[32,128]{1,0:T(8,128)S(1)}) custom-call(f32[1,2,2,3,8,256]{5,4,3,2,1,0:T(8,128)S(1)} %get-tuple-element.52.refs_0_, f32[1,2,2,3,8,256]{5,4,3,2,1,0:T(8,128)S(1)} %get-tuple-element.51.refs_1_, f32[1,2,2,3,8,256]{5,4,3,2,1,0:T(8,128)S(1)} %get-tuple-element.49.refs_2_, ...), custom_call_target="tpu_custom_call" | custom-call | flops 1073741824 | bytes 1048576 | tf_op jit(solution)/shard_map/pallas_call | solution.py:357
  71.3 0.0 collective-permute-done.5.refs_1_
  71.3 1.3 %shard_map.74 = (f32[2,64,256]{2,1,0:T(8,128)}, f32[32,128]{1,0:T(8,128)S(1)}) custom-call(f32[1,2,2,3,8,256]{5,4,3,2,1,0:T(8,128)S(1)} %get-tuple-element.55.refs_0_, f32[1,2,2,3,8,256]{5,4,3,2,1,0:T(8,128)S(1)} %collective-permute-done.5.refs_1_, f32[2,64,256]{2,1,0:T(8,128)} %get-tuple-element.36.refs_2_, ...), custom_call_target="tpu_custom_call", output_to_operand_aliasing={{0}: (2, {}), {1}: (3, {})} | custom-call | flops 1073741824 | bytes 1048576 | tf_op jit(solution)/shard_map/pallas_call | solution.py:357
  72.6 11.6 %all_to_all.9 = f32[32,1,128]{2,1,0:T(1,128)S(1)} all-to-all(f32[32,1,128]{2,1,0:T(1,128)S(1)} %bitcast.7), channel_id=1, replica_groups=mesh['rows'=8,'feat'=4] {'rows','feat'}, dimensions={0} | all-to-all | bytes 32768 | tf_op jit(solution)/shard_map/all_to_all | solution.py:440
  84.1 0.6 reduce_max.9
  (4 shorter events, 0.1 us)
Async XLA Ops:
  11.8 19.2 %collective-permute-start = (f32[4,2,2,3,8,256]{5,4,3,2,1,0:T(8,128)S(1)}, f32[4,2,2,3,8,256]{5,4,3,2,1,0:T(8,128)S(1)}, u32[]{:S(2)}, u32[]{:S(2)}) collective-permute-start(f32[4,2,2,3,8,256]{5,4,3,2,1,0:T(8,128)S(1)} %get-tuple-element.30), channel_id=1, source_target_pairs={{0,4},{4,0},{8,12},{12,8},{16,20},{20,16},{24,28},{28,24},{1,5},{5... | collective-permute-start | bytes 1179656 | tf_op jit(solution)/shard_map/ppermute | solution.py:399
  14.9 0.7 copy-start
  22.3 19.5 %collective-permute-start.6 = (f32[4,2,2,3,8,256]{5,4,3,2,1,0:T(8,128)S(1)}, f32[4,2,2,3,8,256]{5,4,3,2,1,0:T(8,128)S(1)}, u32[]{:S(2)}, u32[]{:S(2)}) collective-permute-start(f32[4,2,2,3,8,256]{5,4,3,2,1,0:T(8,128)S(1)} %get-tuple-element.24), channel_id=1, source_target_pairs={{0,4},{4,0},{8,12},{12,8},{16,20},{20,16},{24,28},{28,24},{1,5},{5... | collective-permute-start | bytes 1179656 | tf_op jit(solution)/shard_map/ppermute | solution.py:399
  22.4 20.5 %collective-permute-start.1 = (f32[4,2,2,3,8,256]{5,4,3,2,1,0:T(8,128)S(1)}, f32[4,2,2,3,8,256]{5,4,3,2,1,0:T(8,128)S(1)}, u32[]{:S(2)}, u32[]{:S(2)}) collective-permute-start(f32[4,2,2,3,8,256]{5,4,3,2,1,0:T(8,128)S(1)} %get-tuple-element.25), channel_id=1, source_target_pairs={{0,4},{4,0},{8,12},{12,8},{16,20},{20,16},{24,28},{28,24},{1,5},{5... | collective-permute-start | bytes 1179656 | tf_op jit(solution)/shard_map/ppermute | solution.py:399
  30.9 22.4 %collective-permute-start.3 = (f32[4,2,2,3,8,256]{5,4,3,2,1,0:T(8,128)S(1)}, f32[4,2,2,3,8,256]{5,4,3,2,1,0:T(8,128)S(1)}, u32[]{:S(2)}, u32[]{:S(2)}) collective-permute-start(f32[4,2,2,3,8,256]{5,4,3,2,1,0:T(8,128)S(1)} %get-tuple-element.27), channel_id=1, source_target_pairs={{0,4},{4,0},{8,12},{12,8},{16,20},{20,16},{24,28},{28,24},{1,5},{5... | collective-permute-start | bytes 1179656 | tf_op jit(solution)/shard_map/ppermute | solution.py:399
  31.1 14.6 %collective-permute-start.2 = (f32[2,2,2,3,8,256]{5,4,3,2,1,0:T(8,128)S(1)}, f32[2,2,2,3,8,256]{5,4,3,2,1,0:T(8,128)S(1)}, u32[]{:S(2)}, u32[]{:S(2)}) collective-permute-start(f32[2,2,2,3,8,256]{5,4,3,2,1,0:T(8,128)S(1)} %get-tuple-element.47), channel_id=1, source_target_pairs={{0,8},{4,12},{8,0},{12,4},{16,24},{20,28},{24,16},{28,20},{1,9},{5... | collective-permute-start | bytes 589832 | tf_op jit(solution)/shard_map/ppermute | solution.py:399
  41.9 12.6 %collective-permute-start.7 = (f32[2,2,2,3,8,256]{5,4,3,2,1,0:T(8,128)S(1)}, f32[2,2,2,3,8,256]{5,4,3,2,1,0:T(8,128)S(1)}, u32[]{:S(2)}, u32[]{:S(2)}) collective-permute-start(f32[2,2,2,3,8,256]{5,4,3,2,1,0:T(8,128)S(1)} %get-tuple-element.43), channel_id=1, source_target_pairs={{0,8},{4,12},{8,0},{12,4},{16,24},{20,28},{24,16},{28,20},{1,9},{5... | collective-permute-start | bytes 589832 | tf_op jit(solution)/shard_map/ppermute | solution.py:399
  42.9 12.5 %collective-permute-start.8 = (f32[2,2,2,3,8,256]{5,4,3,2,1,0:T(8,128)S(1)}, f32[2,2,2,3,8,256]{5,4,3,2,1,0:T(8,128)S(1)}, u32[]{:S(2)}, u32[]{:S(2)}) collective-permute-start(f32[2,2,2,3,8,256]{5,4,3,2,1,0:T(8,128)S(1)} %get-tuple-element.41), channel_id=1, source_target_pairs={{0,8},{4,12},{8,0},{12,4},{16,24},{20,28},{24,16},{28,20},{1,9},{5... | collective-permute-start | bytes 589832 | tf_op jit(solution)/shard_map/ppermute | solution.py:399
  45.8 19.7 %collective-permute-start.9 = (f32[1,2,2,3,8,256]{5,4,3,2,1,0:T(8,128)S(1)}, f32[1,2,2,3,8,256]{5,4,3,2,1,0:T(8,128)S(1)}, u32[]{:S(2)}, u32[]{:S(2)}) collective-permute-start(f32[1,2,2,3,8,256]{5,4,3,2,1,0:T(8,128)S(1)} %get-tuple-element.53), channel_id=1, source_target_pairs={{0,16},{4,20},{8,24},{12,28},{16,0},{20,4},{24,8},{28,12},{1,17},{... | collective-permute-start | bytes 294920 | tf_op jit(solution)/shard_map/ppermute | solution.py:399
  53.3 7.4 %collective-permute-start.4 = (f32[2,2,2,3,8,256]{5,4,3,2,1,0:T(8,128)S(1)}, f32[2,2,2,3,8,256]{5,4,3,2,1,0:T(8,128)S(1)}, u32[]{:S(2)}, u32[]{:S(2)}) collective-permute-start(f32[2,2,2,3,8,256]{5,4,3,2,1,0:T(8,128)S(1)} %get-tuple-element.45), channel_id=1, source_target_pairs={{0,8},{4,12},{8,0},{12,4},{16,24},{20,28},{24,16},{28,20},{1,9},{5... | collective-permute-start | bytes 589832 | tf_op jit(solution)/shard_map/ppermute | solution.py:399
  54.5 10.9 %collective-permute-start.10 = (f32[1,2,2,3,8,256]{5,4,3,2,1,0:T(8,128)S(1)}, f32[1,2,2,3,8,256]{5,4,3,2,1,0:T(8,128)S(1)}, u32[]{:S(2)}, u32[]{:S(2)}) collective-permute-start(f32[1,2,2,3,8,256]{5,4,3,2,1,0:T(8,128)S(1)} %get-tuple-element.50), channel_id=1, source_target_pairs={{0,16},{4,20},{8,24},{12,28},{16,0},{20,4},{24,8},{28,12},{1,17},{... | collective-permute-start | bytes 294920 | tf_op jit(solution)/shard_map/ppermute | solution.py:399
  55.4 13.9 %collective-permute-start.11 = (f32[1,2,2,3,8,256]{5,4,3,2,1,0:T(8,128)S(1)}, f32[1,2,2,3,8,256]{5,4,3,2,1,0:T(8,128)S(1)}, u32[]{:S(2)}, u32[]{:S(2)}) collective-permute-start(f32[1,2,2,3,8,256]{5,4,3,2,1,0:T(8,128)S(1)} %get-tuple-element.48), channel_id=1, source_target_pairs={{0,16},{4,20},{8,24},{12,28},{16,0},{20,4},{24,8},{28,12},{1,17},{... | collective-permute-start | bytes 294920 | tf_op jit(solution)/shard_map/ppermute | solution.py:399
  60.8 10.5 %collective-permute-start.5 = (f32[1,2,2,3,8,256]{5,4,3,2,1,0:T(8,128)S(1)}, f32[1,2,2,3,8,256]{5,4,3,2,1,0:T(8,128)S(1)}, u32[]{:S(2)}, u32[]{:S(2)}) collective-permute-start(f32[1,2,2,3,8,256]{5,4,3,2,1,0:T(8,128)S(1)} %get-tuple-element.54), channel_id=1, source_target_pairs={{0,16},{4,20},{8,24},{12,28},{16,0},{20,4},{24,8},{28,12},{1,17},{... | collective-permute-start | bytes 294920 | tf_op jit(solution)/shard_map/ppermute | solution.py:399
where the time goes:
time: 84.5 us; the launch traced here: 84.7 us
  Pallas kernels  38.6 us (46%)
  starting transfers between devices  26.4 us (31%)
  blocking collectives  11.6 us (14%)
  waiting for transfers between devices  5.91 us (7%)
  other arithmetic  0.89 us (1%)
    ppermute x12, starting transfers between devices, swap(): return lax.ppermute(x, 'rows', [(i, i ^ bit) for i in range(owners)])  26.4 us
    pallas_call x4, Pallas kernels, histogram(): pl.pallas_call(functools.partial(histogram_kernel, first_rows), grid_spec...  24.1 us
    all_to_all x1, blocking collectives, local(): best = lax.all_to_all(best, ('rows', 'feat'), 0, 0, tiled=True)  11.6 us
    pallas_call x1, Pallas kernels, pack(): pl.pallas_call(functools.partial(pack_kernel, blocks, first_rows), grid_s...  11.2 us
    ppermute x12, waiting for transfers between devices, swap(): return lax.ppermute(x, 'rows', [(i, i ^ bit) for i in range(owners)])  5.91 us
    pallas_call x2, Pallas kernels, gain(): pl.pallas_call(functools.partial(gain_kernel, count), grid=(1,), in_specs...  3.29 us
  transfers between devices with their start and end apart: 12, of which 3 were waited for; matrix products, arithmetic and copies ran while one was open for 0% of the time, Pallas kernels for 31%

commit v1 on v0

--- a/solution.py
+++ b/solution.py
@@ -25,7 +25,14 @@
 BIG = 3 * TILE
 SPAN = 512
 WAYS = 4
-PLAN = (([(1,1),(2,1)], []), ([(3,1),(0,0)], [0]), ([(2,0),(1,0)], [2,0]), ([(3,0)], [1,2]), ([], [3,1,3]))
+ORDERS = ((2, 4, 1), (1, 2, 4), (1, 2, 4), (1, 2, 4))
+PLAN = (
+    ([(1, 1), (2, 1)], []),
+    ([(0, 0), (1, 0)], [0, 1]),
+    ([(3, 1), (2, 0)], [1, 2, 0]),
+    ([(3, 0)], [2, 3]),
+    ([], [3]),
+)
 SUMS = (2, LEAVES, STATS, FOLD, WIDTH)
 
 BF = jnp.bfloat16
@@ -177,7 +184,7 @@
             pltpu.VMEM((feat_local, room), BF),
             pltpu.VMEM((STATS, 16, room), BF),
             pltpu.VMEM((WAYS,) + SUMS, F32),
-            jax.ShapeDtypeStruct((8,), jnp.int32),
+            pltpu.SMEM((8,), jnp.int32),
         ],
         compiler_params=pltpu.CompilerParams(vmem_limit_bytes=MOST_VMEM),
         cost_estimate=pl.CostEstimate(flops=4 << 30, bytes_accessed=16 << 20, transcendentals=0),
@@ -272,7 +279,7 @@
         out_shape=[pltpu.VMEM((WAYS,) + SUMS, F32)] * len(jobs),
         compiler_params=pltpu.CompilerParams(vmem_limit_bytes=VMEM_BYTES),
         cost_estimate=pl.CostEstimate(flops=(6 << 30) * len(jobs), bytes_accessed=4 << 20, transcendentals=0),
-    )(info, in_vmem(table), in_vmem(weight))
+    )(pltpu.with_memory_space_constraint(info, pltpu.SMEM), in_vmem(table), in_vmem(weight))
 
 
 def pick(x, chooser):
@@ -391,34 +398,37 @@
     pos = lax.axis_index("rows").astype(jnp.int32)[None]
     room = -(-(row_total + 2 * TILE + BLOCK) // SPAN) * SPAN
     pairs = feat_local // owners // PAIR
-    bits = [1 << b for b in range(1, owners.bit_length() - 1)]
-    kept = in_halves([w for w in range(owners) if not w & 1], bits)
-    parts = [kept[i : i + WAYS] for i in range(0, len(kept), WAYS)]
+    bits = [1 << b for b in range(owners.bit_length() - 1)]
+    plan, orders = PLAN, ORDERS
+    if (owners, pairs) != (8, 4):
+        plan = [([(pair, side)], []) for pair in range(pairs) for side in (1, 0)]
+        plan += [([], [pair for pair in range(pairs) for _ in bits[1:]])]
+        orders = [bits] * pairs
+
+    def ways_of(pair, side):
+        first, *rest = orders[pair]
+        kept = in_halves([w for w in range(owners) if not w & first], rest)
+        kept = [w ^ first for w in kept] if side else kept
+        return [kept[i : i + WAYS] for i in range(0, len(kept), WAYS)]
 
     def swap(x, bit):
         return lax.ppermute(x, "rows", [(i, i ^ bit) for i in range(owners)])
 
-    def ways_of(side, part):
-        return [w ^ side for w in part]
-
-    first_rows = rows_of(feat_local // owners, [(0, ways_of(1, parts[0]))])
+    first_rows = rows_of(feat_local // owners, [(0, ways_of(0, 1)[0])])
     *packed, first, info = pack(
         pos, leaf_of_block, block_rows, bin_codes, gradient, hessian, room, first_rows
     )
     packed = (*packed, info)
-    keep, other, left = {}, {0: [swap(first, 1)]}, {pair: bits for pair in range(pairs)}
-    plan = PLAN
-    if pairs != 4:
-        plan = [([(pair, side)], []) for pair in range(pairs) for side in (1, 0)]
-        plan += [([], [pair for pair in range(pairs) for _ in bits])]
+    keep, other = {}, {0: [swap(first, orders[0][0])]}
+    left = {pair: orders[pair][1:] for pair in range(pairs)}
     for jobs, exchanges in plan:
-        for n, part in enumerate(parts):
+        for n in range(owners // 2 // WAYS):
             todo = [job for job in jobs if n or job != (0, 1)]
             if not todo:
                 continue
-            sums = histogram(packed, owners, [(pair, ways_of(side, part)) for pair, side in todo])
+            sums = histogram(packed, owners, [(pair, ways_of(pair, side)[n]) for pair, side in todo])
             for (pair, side), x in zip(todo, sums):
-                (other if side else keep).setdefault(pair, []).append(swap(x, 1) if side else x)
+                (other if side else keep).setdefault(pair, []).append(swap(x, orders[pair][0]) if side else x)
             packed = in_turn(packed, sums)
         moved = []
         for pair in exchanges:

time: 84.5 us -> 79.7 us (0.943)
  starting transfers between devices: 26.4 us -> 20 us
  waiting for transfers between devices: 5.91 us -> 9.66 us
  Pallas kernels: 38.6 us -> 36 us
    ppermute x12, starting transfers between devices: 26.4 us -> 20 us  [swap(): return lax.ppermute(x, 'rows', [(i, i ^ bit) for i in range(owners)])]
    ppermute x12, waiting for transfers between devices: 5.91 us -> 9.66 us  [swap(): return lax.ppermute(x, 'rows', [(i, i ^ bit) for i in range(owners)])]
    pallas_call x4, Pallas kernels: 24.1 us -> 21.9 us  [histogram(): pl.pallas_call(functools.partial(histogram_kernel, first_rows), grid_spec...]
    all_to_all x1, blocking collectives: 11.6 us -> 12.4 us  [local(): best = lax.all_to_all(best, ('rows', 'feat'), 0, 0, tiled=True)]
  transfers between devices with their start and end apart: 12 -> 12, of which waited for: 3 -> 4; matrix products, arithmetic and copies ran while one was open for 0% -> 0% of each run, Pallas kernels for 31% -> 30%
where the time goes in v1:
time: 79.7 us
  Pallas kernels  36 us (45%)
  starting transfers between devices  20 us (25%)
  blocking collectives  12.4 us (16%)
  waiting for transfers between devices  9.66 us (12%)
  other arithmetic  0.87 us (1%)
    pallas_call x4, Pallas kernels, histogram(): pl.pallas_call(functools.partial(histogram_kernel, first_rows), grid_spec...  21.9 us
    ppermute x12, starting transfers between devices, swap(): return lax.ppermute(x, 'rows', [(i, i ^ bit) for i in range(owners)])  20 us
    all_to_all x1, blocking collectives, local(): best = lax.all_to_all(best, ('rows', 'feat'), 0, 0, tiled=True)  12.4 us
    pallas_call x1, Pallas kernels, pack(): pl.pallas_call(functools.partial(pack_kernel, blocks, first_rows), grid_s...  10.9 us
    ppermute x12, waiting for transfers between devices, swap(): return lax.ppermute(x, 'rows', [(i, i ^ bit) for i in range(owners)])  9.66 us
    pallas_call x2, Pallas kernels, gain(): pl.pallas_call(functools.partial(gain_kernel, count), grid=(1,), in_specs...  3.28 us
  transfers between devices with their start and end apart: 12, of which 4 were waited for; matrix products, arithmetic and copies ran while one was open for 0% of the time, Pallas kernels for 30%

profile of v1, /device:TPU:0, one launch (start us, length us, event | category | flops | bytes accessed | tf_op | source)
XLA Modules:
  0.0 79.7 jit_solution(8760784032686768917)
XLA Ops:
  0.6 10.9 %shard_map.68 = (bf16[512,5120]{1,0:T(8,128)(2,1)S(1)}, bf16[3,16,5120]{2,1,0:T(8,128)(2,1)S(1)}, f32[4,2,2,3,8,256]{5,4,3,2,1,0:T(8,128)S(1)}, s32[8]{0:T(128)S(4)}) custom-call(s32[1]{0:T(128)} %bitcast.pos_ref, s32[32]{0:T(128)} %leaf_ref.1, s32[32]{0:T(128)} %rows_ref.1, s32[4096,512]{1,0:T(8,128)} %codes_ref.1, bf16[32,128]{1,0:T(8,128)(2,1)} %bitcast.9, ...), custom_call_target="tpu_custom_call" | custom-call | flops 4294967296 | bytes 16777216 | tf_op jit(solution)/shard_map/pallas_call | solution.py:164
  11.5 3.1 %collective-permute-start = (f32[4,2,2,3,8,256]{5,4,3,2,1,0:T(8,128)S(1)}, f32[4,2,2,3,8,256]{5,4,3,2,1,0:T(8,128)S(1)}, u32[]{:S(2)}, u32[]{:S(2)}) collective-permute-start(f32[4,2,2,3,8,256]{5,4,3,2,1,0:T(8,128)S(1)} %get-tuple-element.30), channel_id=1, source_target_pairs={{0,8},{4,12},{8,0},{12,4},{16,24},{20,28},{24,16},{28,20},{1,9},{5... | collective-permute-start | bytes 1179656 | tf_op jit(solution)/shard_map/ppermute | solution.py:415
  14.6 6.2 %shard_map.69 = (f32[4,2,2,3,8,256]{5,4,3,2,1,0:T(8,128)S(1)}, f32[4,2,2,3,8,256]{5,4,3,2,1,0:T(8,128)S(1)}) custom-call(s32[8]{0:T(128)S(4)} %get-tuple-element.35.info_ref, bf16[512,5120]{1,0:T(8,128)(2,1)S(1)} %get-tuple-element.22.table_ref, bf16[3,16,5120]{2,1,0:T(8,128)(2,1)S(1)} %get-tuple-element.23.weight_ref), custom_call_target="tpu_custom_call" | custom-call | flops 12884901888 | bytes 4194304 | tf_op jit(solution)/shard_map/pallas_call | solution.py:270
  20.8 3.5 %collective-permute-start.1 = (f32[4,2,2,3,8,256]{5,4,3,2,1,0:T(8,128)S(1)}, f32[4,2,2,3,8,256]{5,4,3,2,1,0:T(8,128)S(1)}, u32[]{:S(2)}, u32[]{:S(2)}) collective-permute-start(f32[4,2,2,3,8,256]{5,4,3,2,1,0:T(8,128)S(1)} %get-tuple-element.24), channel_id=1, source_target_pairs={{0,4},{4,0},{8,12},{12,8},{16,20},{20,16},{24,28},{28,24},{1,5},{5... | collective-permute-start | bytes 1179656 | tf_op jit(solution)/shard_map/ppermute | solution.py:415
  24.3 0.1 collective-permute-start.3
  24.4 6.0 %shard_map.70 = (f32[4,2,2,3,8,256]{5,4,3,2,1,0:T(8,128)S(1)}, f32[4,2,2,3,8,256]{5,4,3,2,1,0:T(8,128)S(1)}) custom-call(s32[8]{0:T(128)S(4)} %get-tuple-element.35.info_ref, bf16[512,5120]{1,0:T(8,128)(2,1)S(1)} %get-tuple-element.22.table_ref, bf16[3,16,5120]{2,1,0:T(8,128)(2,1)S(1)} %get-tuple-element.23.weight_ref), custom_call_target="tpu_custom_call" | custom-call | flops 12884901888 | bytes 4194304 | tf_op jit(solution)/shard_map/pallas_call | solution.py:270
  30.4 3.9 %collective-permute-done.1 = f32[4,2,2,3,8,256]{5,4,3,2,1,0:T(8,128)S(1)} collective-permute-done((f32[4,2,2,3,8,256]{5,4,3,2,1,0:T(8,128)S(1)}, f32[4,2,2,3,8,256]{5,4,3,2,1,0:T(8,128)S(1)}, u32[]{:S(2)}, u32[]{:S(2)}) %collective-permute-start.1) | collective-permute-done | bytes 393248 | tf_op jit(solution)/shard_map/ppermute | solution.py:415
  34.3 0.1 slice_add_fusion.5
  34.4 0.3 collective-permute-start.2
  34.7 0.0 collective-permute-done
  34.7 0.1 slice_add_fusion.3
  34.8 2.6 %collective-permute-start.4 = (f32[2,2,2,3,8,256]{5,4,3,2,1,0:T(8,128)S(1)}, f32[2,2,2,3,8,256]{5,4,3,2,1,0:T(8,128)S(1)}, u32[]{:S(2)}, u32[]{:S(2)}) collective-permute-start(f32[2,2,2,3,8,256]{5,4,3,2,1,0:T(8,128)S(1)} %get-tuple-element.45), channel_id=1, source_target_pairs={{0,16},{4,20},{8,24},{12,28},{16,0},{20,4},{24,8},{28,12},{1,17},{... | collective-permute-start | bytes 589832 | tf_op jit(solution)/shard_map/ppermute | solution.py:415
  37.4 6.2 %shard_map.71 = (f32[4,2,2,3,8,256]{5,4,3,2,1,0:T(8,128)S(1)}, f32[4,2,2,3,8,256]{5,4,3,2,1,0:T(8,128)S(1)}) custom-call(s32[8]{0:T(128)S(4)} %get-tuple-element.35.info_ref, bf16[512,5120]{1,0:T(8,128)(2,1)S(1)} %get-tuple-element.22.table_ref, bf16[3,16,5120]{2,1,0:T(8,128)(2,1)S(1)} %get-tuple-element.23.weight_ref), custom_call_target="tpu_custom_call" | custom-call | flops 12884901888 | bytes 4194304 | tf_op jit(solution)/shard_map/pallas_call | solution.py:270
  43.6 2.3 %collective-permute-start.5 = (f32[4,2,2,3,8,256]{5,4,3,2,1,0:T(8,128)S(1)}, f32[4,2,2,3,8,256]{5,4,3,2,1,0:T(8,128)S(1)}, u32[]{:S(2)}, u32[]{:S(2)}) collective-permute-start(f32[4,2,2,3,8,256]{5,4,3,2,1,0:T(8,128)S(1)} %get-tuple-element.32), channel_id=1, source_target_pairs={{0,4},{4,0},{8,12},{12,8},{16,20},{20,16},{24,28},{28,24},{1,5},{5... | collective-permute-start | bytes 1179656 | tf_op jit(solution)/shard_map/ppermute | solution.py:415
  45.9 0.0 collective-permute-done.3
  45.9 0.1 slice_add_fusion
  46.0 1.8 %collective-permute-start.8 = (f32[2,2,2,3,8,256]{5,4,3,2,1,0:T(8,128)S(1)}, f32[2,2,2,3,8,256]{5,4,3,2,1,0:T(8,128)S(1)}, u32[]{:S(2)}, u32[]{:S(2)}) collective-permute-start(f32[2,2,2,3,8,256]{5,4,3,2,1,0:T(8,128)S(1)} %get-tuple-element.41), channel_id=1, source_target_pairs={{0,8},{4,12},{8,0},{12,4},{16,24},{20,28},{24,16},{28,20},{1,9},{5... | collective-permute-start | bytes 589832 | tf_op jit(solution)/shard_map/ppermute | solution.py:415
  47.8 0.0 collective-permute-done.2
  47.9 0.7 collective-permute-start.10
  48.5 0.0 collective-permute-done.4
  48.6 0.3 collective-permute-start.9
  48.9 3.5 %shard_map.72 = f32[4,2,2,3,8,256]{5,4,3,2,1,0:T(8,128)S(1)} custom-call(s32[8]{0:T(128)S(4)} %get-tuple-element.35.info_ref, bf16[512,5120]{1,0:T(8,128)(2,1)S(1)} %get-tuple-element.22.table_ref, bf16[3,16,5120]{2,1,0:T(8,128)(2,1)S(1)} %get-tuple-element.23.weight_ref), custom_call_target="tpu_custom_call" | custom-call | flops 6442450944 | bytes 4194304 | tf_op jit(solution)/shard_map/pallas_call | solution.py:270
  52.4 0.5 collective-permute-done.5
  52.9 0.1 slice_add_fusion.2
  53.0 1.8 %collective-permute-start.6 = (f32[2,2,2,3,8,256]{5,4,3,2,1,0:T(8,128)S(1)}, f32[2,2,2,3,8,256]{5,4,3,2,1,0:T(8,128)S(1)}, u32[]{:S(2)}, u32[]{:S(2)}) collective-permute-start(f32[2,2,2,3,8,256]{5,4,3,2,1,0:T(8,128)S(1)} %get-tuple-element.43), channel_id=1, source_target_pairs={{0,8},{4,12},{8,0},{12,4},{16,24},{20,28},{24,16},{28,20},{1,9},{5... | collective-permute-start | bytes 589832 | tf_op jit(solution)/shard_map/ppermute | solution.py:415
  54.7 0.0 collective-permute-done.8
  54.8 1.2 %collective-permute-start.11 = (f32[1,2,2,3,8,256]{5,4,3,2,1,0:T(8,128)S(1)}, f32[1,2,2,3,8,256]{5,4,3,2,1,0:T(8,128)S(1)}, u32[]{:S(2)}, u32[]{:S(2)}) collective-permute-start(f32[1,2,2,3,8,256]{5,4,3,2,1,0:T(8,128)S(1)} %get-tuple-element.48), channel_id=1, source_target_pairs={{0,16},{4,20},{8,24},{12,28},{16,0},{20,4},{24,8},{28,12},{1,17},{... | collective-permute-start | bytes 294920 | tf_op jit(solution)/shard_map/ppermute | solution.py:415
  56.0 3.0 %collective-permute-done.6 = f32[2,2,2,3,8,256]{5,4,3,2,1,0:T(8,128)S(1)} collective-permute-done((f32[2,2,2,3,8,256]{5,4,3,2,1,0:T(8,128)S(1)}, f32[2,2,2,3,8,256]{5,4,3,2,1,0:T(8,128)S(1)}, u32[]{:S(2)}, u32[]{:S(2)}) %collective-permute-start.6) | collective-permute-done | bytes 196640 | tf_op jit(solution)/shard_map/ppermute | solution.py:415
  59.0 2.2 %collective-permute-start.7 = (f32[1,2,2,3,8,256]{5,4,3,2,1,0:T(8,128)S(1)}, f32[1,2,2,3,8,256]{5,4,3,2,1,0:T(8,128)S(1)}, u32[]{:S(2)}, u32[]{:S(2)}) collective-permute-start(f32[1,2,2,3,8,256]{5,4,3,2,1,0:T(8,128)S(1)} %get-tuple-element.54), channel_id=1, source_target_pairs={{0,16},{4,20},{8,24},{12,28},{16,0},{20,4},{24,8},{28,12},{1,17},{... | collective-permute-start | bytes 294920 | tf_op jit(solution)/shard_map/ppermute | solution.py:415
  61.2 0.0 collective-permute-done.10.refs_4_
  61.2 0.0 collective-permute-done.9.refs_3_
  61.2 2.3 %collective-permute-done.11.refs_5_ = f32[1,2,2,3,8,256]{5,4,3,2,1,0:T(8,128)S(1)} collective-permute-done((f32[1,2,2,3,8,256]{5,4,3,2,1,0:T(8,128)S(1)}, f32[1,2,2,3,8,256]{5,4,3,2,1,0:T(8,128)S(1)}, u32[]{:S(2)}, u32[]{:S(2)}) %collective-permute-start.11) | collective-permute-done | bytes 98336 | tf_op jit(solution)/shard_map/ppermute | solution.py:415
  63.5 2.0 %shard_map.73 = (f32[2,64,256]{2,1,0:T(8,128)}, f32[32,128]{1,0:T(8,128)S(1)}) custom-call(f32[1,2,2,3,8,256]{5,4,3,2,1,0:T(8,128)S(1)} %get-tuple-element.52.refs_0_, f32[1,2,2,3,8,256]{5,4,3,2,1,0:T(8,128)S(1)} %get-tuple-element.50.refs_1_, f32[1,2,2,3,8,256]{5,4,3,2,1,0:T(8,128)S(1)} %get-tuple-element.49.refs_2_, ...), custom_call_target="tpu_custom_call" | custom-call | flops 1073741824 | bytes 1048576 | tf_op jit(solution)/shard_map/pallas_call | solution.py:364
  65.5 0.0 collective-permute-done.7.refs_1_
  65.5 1.3 %shard_map.74 = (f32[2,64,256]{2,1,0:T(8,128)}, f32[32,128]{1,0:T(8,128)S(1)}) custom-call(f32[1,2,2,3,8,256]{5,4,3,2,1,0:T(8,128)S(1)} %get-tuple-element.55.refs_0_, f32[1,2,2,3,8,256]{5,4,3,2,1,0:T(8,128)S(1)} %collective-permute-done.7.refs_1_, f32[2,64,256]{2,1,0:T(8,128)} %get-tuple-element.36.refs_2_, ...), custom_call_target="tpu_custom_call", output_to_operand_aliasing={{0}: (2, {}), {1}: (3, {})} | custom-call | flops 1073741824 | bytes 1048576 | tf_op jit(solution)/shard_map/pallas_call | solution.py:364
  66.8 12.4 %all_to_all.9 = f32[32,1,128]{2,1,0:T(1,128)S(1)} all-to-all(f32[32,1,128]{2,1,0:T(1,128)S(1)} %bitcast.7), channel_id=1, replica_groups=mesh['rows'=8,'feat'=4] {'rows','feat'}, dimensions={0} | all-to-all | bytes 32768 | tf_op jit(solution)/shard_map/all_to_all | solution.py:450
  79.2 0.6 reduce_max.9
  (4 shorter events, 0.1 us)
Async XLA Ops:
  11.5 23.2 %collective-permute-start = (f32[4,2,2,3,8,256]{5,4,3,2,1,0:T(8,128)S(1)}, f32[4,2,2,3,8,256]{5,4,3,2,1,0:T(8,128)S(1)}, u32[]{:S(2)}, u32[]{:S(2)}) collective-permute-start(f32[4,2,2,3,8,256]{5,4,3,2,1,0:T(8,128)S(1)} %get-tuple-element.30), channel_id=1, source_target_pairs={{0,8},{4,12},{8,0},{12,4},{16,24},{20,28},{24,16},{28,20},{1,9},{5... | collective-permute-start | bytes 1179656 | tf_op jit(solution)/shard_map/ppermute | solution.py:415
  20.8 13.5 %collective-permute-start.1 = (f32[4,2,2,3,8,256]{5,4,3,2,1,0:T(8,128)S(1)}, f32[4,2,2,3,8,256]{5,4,3,2,1,0:T(8,128)S(1)}, u32[]{:S(2)}, u32[]{:S(2)}) collective-permute-start(f32[4,2,2,3,8,256]{5,4,3,2,1,0:T(8,128)S(1)} %get-tuple-element.24), channel_id=1, source_target_pairs={{0,4},{4,0},{8,12},{12,8},{16,20},{20,16},{24,28},{28,24},{1,5},{5... | collective-permute-start | bytes 1179656 | tf_op jit(solution)/shard_map/ppermute | solution.py:415
  24.3 21.6 %collective-permute-start.3 = (f32[4,2,2,3,8,256]{5,4,3,2,1,0:T(8,128)S(1)}, f32[4,2,2,3,8,256]{5,4,3,2,1,0:T(8,128)S(1)}, u32[]{:S(2)}, u32[]{:S(2)}) collective-permute-start(f32[4,2,2,3,8,256]{5,4,3,2,1,0:T(8,128)S(1)} %get-tuple-element.25), channel_id=1, source_target_pairs={{0,4},{4,0},{8,12},{12,8},{16,20},{20,16},{24,28},{28,24},{1,5},{5... | collective-permute-start | bytes 1179656 | tf_op jit(solution)/shard_map/ppermute | solution.py:415
  34.4 13.5 %collective-permute-start.2 = (f32[2,2,2,3,8,256]{5,4,3,2,1,0:T(8,128)S(1)}, f32[2,2,2,3,8,256]{5,4,3,2,1,0:T(8,128)S(1)}, u32[]{:S(2)}, u32[]{:S(2)}) collective-permute-start(f32[2,2,2,3,8,256]{5,4,3,2,1,0:T(8,128)S(1)} %get-tuple-element.47), channel_id=1, source_target_pairs={{0,8},{4,12},{8,0},{12,4},{16,24},{20,28},{24,16},{28,20},{1,9},{5... | collective-permute-start | bytes 589832 | tf_op jit(solution)/shard_map/ppermute | solution.py:415
  34.8 13.8 %collective-permute-start.4 = (f32[2,2,2,3,8,256]{5,4,3,2,1,0:T(8,128)S(1)}, f32[2,2,2,3,8,256]{5,4,3,2,1,0:T(8,128)S(1)}, u32[]{:S(2)}, u32[]{:S(2)}) collective-permute-start(f32[2,2,2,3,8,256]{5,4,3,2,1,0:T(8,128)S(1)} %get-tuple-element.45), channel_id=1, source_target_pairs={{0,16},{4,20},{8,24},{12,28},{16,0},{20,4},{24,8},{28,12},{1,17},{... | collective-permute-start | bytes 589832 | tf_op jit(solution)/shard_map/ppermute | solution.py:415
  43.6 9.3 %collective-permute-start.5 = (f32[4,2,2,3,8,256]{5,4,3,2,1,0:T(8,128)S(1)}, f32[4,2,2,3,8,256]{5,4,3,2,1,0:T(8,128)S(1)}, u32[]{:S(2)}, u32[]{:S(2)}) collective-permute-start(f32[4,2,2,3,8,256]{5,4,3,2,1,0:T(8,128)S(1)} %get-tuple-element.32), channel_id=1, source_target_pairs={{0,4},{4,0},{8,12},{12,8},{16,20},{20,16},{24,28},{28,24},{1,5},{5... | collective-permute-start | bytes 1179656 | tf_op jit(solution)/shard_map/ppermute | solution.py:415
  46.0 8.7 %collective-permute-start.8 = (f32[2,2,2,3,8,256]{5,4,3,2,1,0:T(8,128)S(1)}, f32[2,2,2,3,8,256]{5,4,3,2,1,0:T(8,128)S(1)}, u32[]{:S(2)}, u32[]{:S(2)}) collective-permute-start(f32[2,2,2,3,8,256]{5,4,3,2,1,0:T(8,128)S(1)} %get-tuple-element.41), channel_id=1, source_target_pairs={{0,8},{4,12},{8,0},{12,4},{16,24},{20,28},{24,16},{28,20},{1,9},{5... | collective-permute-start | bytes 589832 | tf_op jit(solution)/shard_map/ppermute | solution.py:415
  47.9 13.3 %collective-permute-start.10 = (f32[1,2,2,3,8,256]{5,4,3,2,1,0:T(8,128)S(1)}, f32[1,2,2,3,8,256]{5,4,3,2,1,0:T(8,128)S(1)}, u32[]{:S(2)}, u32[]{:S(2)}) collective-permute-start(f32[1,2,2,3,8,256]{5,4,3,2,1,0:T(8,128)S(1)} %get-tuple-element.51), channel_id=1, source_target_pairs={{0,16},{4,20},{8,24},{12,28},{16,0},{20,4},{24,8},{28,12},{1,17},{... | collective-permute-start | bytes 294920 | tf_op jit(solution)/shard_map/ppermute | solution.py:415
  48.6 12.6 %collective-permute-start.9 = (f32[1,2,2,3,8,256]{5,4,3,2,1,0:T(8,128)S(1)}, f32[1,2,2,3,8,256]{5,4,3,2,1,0:T(8,128)S(1)}, u32[]{:S(2)}, u32[]{:S(2)}) collective-permute-start(f32[1,2,2,3,8,256]{5,4,3,2,1,0:T(8,128)S(1)} %get-tuple-element.53), channel_id=1, source_target_pairs={{0,4},{4,0},{8,12},{12,8},{16,20},{20,16},{24,28},{28,24},{1,5},{5... | collective-permute-start | bytes 294920 | tf_op jit(solution)/shard_map/ppermute | solution.py:415
  53.0 6.0 %collective-permute-start.6 = (f32[2,2,2,3,8,256]{5,4,3,2,1,0:T(8,128)S(1)}, f32[2,2,2,3,8,256]{5,4,3,2,1,0:T(8,128)S(1)}, u32[]{:S(2)}, u32[]{:S(2)}) collective-permute-start(f32[2,2,2,3,8,256]{5,4,3,2,1,0:T(8,128)S(1)} %get-tuple-element.43), channel_id=1, source_target_pairs={{0,8},{4,12},{8,0},{12,4},{16,24},{20,28},{24,16},{28,20},{1,9},{5... | collective-permute-start | bytes 589832 | tf_op jit(solution)/shard_map/ppermute | solution.py:415
  54.8 8.7 %collective-permute-start.11 = (f32[1,2,2,3,8,256]{5,4,3,2,1,0:T(8,128)S(1)}, f32[1,2,2,3,8,256]{5,4,3,2,1,0:T(8,128)S(1)}, u32[]{:S(2)}, u32[]{:S(2)}) collective-permute-start(f32[1,2,2,3,8,256]{5,4,3,2,1,0:T(8,128)S(1)} %get-tuple-element.48), channel_id=1, source_target_pairs={{0,16},{4,20},{8,24},{12,28},{16,0},{20,4},{24,8},{28,12},{1,17},{... | collective-permute-start | bytes 294920 | tf_op jit(solution)/shard_map/ppermute | solution.py:415
  59.0 6.5 %collective-permute-start.7 = (f32[1,2,2,3,8,256]{5,4,3,2,1,0:T(8,128)S(1)}, f32[1,2,2,3,8,256]{5,4,3,2,1,0:T(8,128)S(1)}, u32[]{:S(2)}, u32[]{:S(2)}) collective-permute-start(f32[1,2,2,3,8,256]{5,4,3,2,1,0:T(8,128)S(1)} %get-tuple-element.54), channel_id=1, source_target_pairs={{0,16},{4,20},{8,24},{12,28},{16,0},{20,4},{24,8},{28,12},{1,17},{... | collective-permute-start | bytes 294920 | tf_op jit(solution)/shard_map/ppermute | solution.py:415

commit v2 on v1

--- a/solution.py
+++ b/solution.py
@@ -421,7 +421,15 @@
     packed = (*packed, info)
     keep, other = {}, {0: [swap(first, orders[0][0])]}
     left = {pair: orders[pair][1:] for pair in range(pairs)}
+    early, done = range(pairs // 2), ()
+
+    def gain_of(group):
+        return gain([keep[p] for p in group], [other[p] for p in group], group[0], feat_local // owners, devices, done)
+
     for jobs, exchanges in plan:
+        if early and not (done or jobs or any(left[pair] for pair in early)):
+            done = gain_of(early)
+            packed = in_turn(packed, done[1:])
         for n in range(owners // 2 // WAYS):
             todo = [job for job in jobs if n or job != (0, 1)]
             if not todo:
@@ -440,13 +448,9 @@
             moved.append(on)
             keep[pair], other[pair] = mine[:half] + theirs[:half], swap(on, bit)
         packed = in_turn(packed, moved)
-    done = ()
-    for group in (range(pairs - 1), range(pairs - 1, pairs)):
-        if group:
-            done = gain(
-                [keep[p] for p in group], [other[p] for p in group], group[0], feat_local // owners, devices, done
-            )
-    split_gain, best = done
+    if early and not done:
+        done = gain_of(early)
+    split_gain, best = gain_of(range(pairs // 2, pairs))
     best = lax.all_to_all(best, ("rows", "feat"), 0, 0, tiled=True)
     return split_gain, jnp.max(best, axis=0)[:LEAVES]
 

time: 79.7 us -> 80.6 us (1.011)
  Pallas kernels: 36 us -> 39.5 us
  waiting for transfers between devices: 9.66 us -> 7.73 us
  starting transfers between devices: 20 us -> 18.3 us
    pallas_call x4, Pallas kernels: 21.9 us -> 24.6 us  [histogram(): pl.pallas_call(functools.partial(histogram_kernel, first_rows), grid_spec...]
    ppermute x12, waiting for transfers between devices: 9.66 us -> 7.73 us  [swap(): return lax.ppermute(x, 'rows', [(i, i ^ bit) for i in range(owners)])]
    ppermute x12, starting transfers between devices: 20 us -> 18.3 us  [swap(): return lax.ppermute(x, 'rows', [(i, i ^ bit) for i in range(owners)])]
  transfers between devices with their start and end apart: 12 -> 12, of which waited for: 4 -> 4; matrix products, arithmetic and copies ran while one was open for 0% -> 0% of each run, Pallas kernels for 30% -> 33%
where the time goes in v2:
time: 80.6 us; the launch traced here: 80.3 us
  Pallas kernels  39.5 us (49%)
  starting transfers between devices  18.3 us (23%)
  blocking collectives  13.1 us (16%)
  waiting for transfers between devices  7.73 us (10%)
  other arithmetic  0.87 us (1%)
    pallas_call x4, Pallas kernels, histogram(): pl.pallas_call(functools.partial(histogram_kernel, first_rows), grid_spec...  24.6 us
    ppermute x12, starting transfers between devices, swap(): return lax.ppermute(x, 'rows', [(i, i ^ bit) for i in range(owners)])  18.3 us
    all_to_all x1, blocking collectives, local(): best = lax.all_to_all(best, ('rows', 'feat'), 0, 0, tiled=True)  13.1 us
    pallas_call x1, Pallas kernels, pack(): pl.pallas_call(functools.partial(pack_kernel, blocks, first_rows), grid_s...  11.6 us
    ppermute x12, waiting for transfers between devices, swap(): return lax.ppermute(x, 'rows', [(i, i ^ bit) for i in range(owners)])  7.73 us
    pallas_call x2, Pallas kernels, gain(): pl.pallas_call(functools.partial(gain_kernel, count), grid=(1,), in_specs...  3.31 us
  transfers between devices with their start and end apart: 12, of which 4 were waited for; matrix products, arithmetic and copies ran while one was open for 0% of the time, Pallas kernels for 33%

profile of v2, /device:TPU:0, one launch (start us, length us, event | category | flops | bytes accessed | tf_op | source)
XLA Modules:
  0.0 80.3 jit_solution(2114638117117366203)
XLA Ops:
  0.6 11.6 %shard_map.68 = (bf16[512,5120]{1,0:T(8,128)(2,1)S(1)}, bf16[3,16,5120]{2,1,0:T(8,128)(2,1)S(1)}, f32[4,2,2,3,8,256]{5,4,3,2,1,0:T(8,128)S(1)}, s32[8]{0:T(128)S(4)}) custom-call(s32[1]{0:T(128)} %bitcast.pos_ref, s32[32]{0:T(128)} %leaf_ref.1, s32[32]{0:T(128)} %rows_ref.1, s32[4096,512]{1,0:T(8,128)} %codes_ref.1, bf16[32,128]{1,0:T(8,128)(2,1)} %bitcast.9, ...), custom_call_target="tpu_custom_call" | custom-call | flops 4294967296 | bytes 16777216 | tf_op jit(solution)/shard_map/pallas_call | solution.py:164
  12.2 3.1 %collective-permute-start = (f32[4,2,2,3,8,256]{5,4,3,2,1,0:T(8,128)S(1)}, f32[4,2,2,3,8,256]{5,4,3,2,1,0:T(8,128)S(1)}, u32[]{:S(2)}, u32[]{:S(2)}) collective-permute-start(f32[4,2,2,3,8,256]{5,4,3,2,1,0:T(8,128)S(1)} %get-tuple-element.30), channel_id=1, source_target_pairs={{0,8},{4,12},{8,0},{12,4},{16,24},{20,28},{24,16},{28,20},{1,9},{5... | collective-permute-start | bytes 1179656 | tf_op jit(solution)/shard_map/ppermute | solution.py:415
  15.3 6.9 %shard_map.69 = (f32[4,2,2,3,8,256]{5,4,3,2,1,0:T(8,128)S(1)}, f32[4,2,2,3,8,256]{5,4,3,2,1,0:T(8,128)S(1)}) custom-call(s32[8]{0:T(128)S(4)} %get-tuple-element.35.info_ref, bf16[512,5120]{1,0:T(8,128)(2,1)S(1)} %get-tuple-element.22.table_ref, bf16[3,16,5120]{2,1,0:T(8,128)(2,1)S(1)} %get-tuple-element.23.weight_ref), custom_call_target="tpu_custom_call" | custom-call | flops 12884901888 | bytes 4194304 | tf_op jit(solution)/shard_map/pallas_call | solution.py:270
  22.3 0.8 %collective-permute-start.1 = (f32[4,2,2,3,8,256]{5,4,3,2,1,0:T(8,128)S(1)}, f32[4,2,2,3,8,256]{5,4,3,2,1,0:T(8,128)S(1)}, u32[]{:S(2)}, u32[]{:S(2)}) collective-permute-start(f32[4,2,2,3,8,256]{5,4,3,2,1,0:T(8,128)S(1)} %get-tuple-element.24), channel_id=1, source_target_pairs={{0,4},{4,0},{8,12},{12,8},{16,20},{20,16},{24,28},{28,24},{1,5},{5... | collective-permute-start | bytes 1179656 | tf_op jit(solution)/shard_map/ppermute | solution.py:415
  23.1 1.3 %collective-permute-start.2 = (f32[4,2,2,3,8,256]{5,4,3,2,1,0:T(8,128)S(1)}, f32[4,2,2,3,8,256]{5,4,3,2,1,0:T(8,128)S(1)}, u32[]{:S(2)}, u32[]{:S(2)}) collective-permute-start(f32[4,2,2,3,8,256]{5,4,3,2,1,0:T(8,128)S(1)} %get-tuple-element.25), channel_id=1, source_target_pairs={{0,4},{4,0},{8,12},{12,8},{16,20},{20,16},{24,28},{28,24},{1,5},{5... | collective-permute-start | bytes 1179656 | tf_op jit(solution)/shard_map/ppermute | solution.py:415
  24.4 6.8 %shard_map.70 = (f32[4,2,2,3,8,256]{5,4,3,2,1,0:T(8,128)S(1)}, f32[4,2,2,3,8,256]{5,4,3,2,1,0:T(8,128)S(1)}) custom-call(s32[8]{0:T(128)S(4)} %get-tuple-element.35.info_ref, bf16[512,5120]{1,0:T(8,128)(2,1)S(1)} %get-tuple-element.22.table_ref, bf16[3,16,5120]{2,1,0:T(8,128)(2,1)S(1)} %get-tuple-element.23.weight_ref), custom_call_target="tpu_custom_call" | custom-call | flops 12884901888 | bytes 4194304 | tf_op jit(solution)/shard_map/pallas_call | solution.py:270
  31.1 3.3 %collective-permute-done.1 = f32[4,2,2,3,8,256]{5,4,3,2,1,0:T(8,128)S(1)} collective-permute-done((f32[4,2,2,3,8,256]{5,4,3,2,1,0:T(8,128)S(1)}, f32[4,2,2,3,8,256]{5,4,3,2,1,0:T(8,128)S(1)}, u32[]{:S(2)}, u32[]{:S(2)}) %collective-permute-start.1) | collective-permute-done | bytes 393248 | tf_op jit(solution)/shard_map/ppermute | solution.py:415
  34.4 0.1 slice_add_fusion.3
  34.4 0.1 collective-permute-start.4
  34.5 0.0 collective-permute-done
  34.5 0.1 slice_add_fusion.2
  34.6 3.1 %collective-permute-start.5 = (f32[2,2,2,3,8,256]{5,4,3,2,1,0:T(8,128)S(1)}, f32[2,2,2,3,8,256]{5,4,3,2,1,0:T(8,128)S(1)}, u32[]{:S(2)}, u32[]{:S(2)}) collective-permute-start(f32[2,2,2,3,8,256]{5,4,3,2,1,0:T(8,128)S(1)} %get-tuple-element.43), channel_id=1, source_target_pairs={{0,16},{4,20},{8,24},{12,28},{16,0},{20,4},{24,8},{28,12},{1,17},{... | collective-permute-start | bytes 589832 | tf_op jit(solution)/shard_map/ppermute | solution.py:415
  37.7 7.0 %shard_map.71 = (f32[4,2,2,3,8,256]{5,4,3,2,1,0:T(8,128)S(1)}, f32[4,2,2,3,8,256]{5,4,3,2,1,0:T(8,128)S(1)}) custom-call(s32[8]{0:T(128)S(4)} %get-tuple-element.35.info_ref, bf16[512,5120]{1,0:T(8,128)(2,1)S(1)} %get-tuple-element.22.table_ref, bf16[3,16,5120]{2,1,0:T(8,128)(2,1)S(1)} %get-tuple-element.23.weight_ref), custom_call_target="tpu_custom_call" | custom-call | flops 12884901888 | bytes 4194304 | tf_op jit(solution)/shard_map/pallas_call | solution.py:270
  44.7 1.0 %collective-permute-start.6 = (f32[4,2,2,3,8,256]{5,4,3,2,1,0:T(8,128)S(1)}, f32[4,2,2,3,8,256]{5,4,3,2,1,0:T(8,128)S(1)}, u32[]{:S(2)}, u32[]{:S(2)}) collective-permute-start(f32[4,2,2,3,8,256]{5,4,3,2,1,0:T(8,128)S(1)} %get-tuple-element.33), channel_id=1, source_target_pairs={{0,4},{4,0},{8,12},{12,8},{16,20},{20,16},{24,28},{28,24},{1,5},{5... | collective-permute-start | bytes 1179656 | tf_op jit(solution)/shard_map/ppermute | solution.py:415
  45.7 0.0 collective-permute-done.2
  45.7 0.1 slice_add_fusion.5
  45.7 0.9 %collective-permute-start.3 = (f32[2,2,2,3,8,256]{5,4,3,2,1,0:T(8,128)S(1)}, f32[2,2,2,3,8,256]{5,4,3,2,1,0:T(8,128)S(1)}, u32[]{:S(2)}, u32[]{:S(2)}) collective-permute-start(f32[2,2,2,3,8,256]{5,4,3,2,1,0:T(8,128)S(1)} %get-tuple-element.47), channel_id=1, source_target_pairs={{0,8},{4,12},{8,0},{12,4},{16,24},{20,28},{24,16},{28,20},{1,9},{5... | collective-permute-start | bytes 589832 | tf_op jit(solution)/shard_map/ppermute | solution.py:415
  46.6 0.0 collective-permute-done.4
  46.7 0.6 collective-permute-start.11
  47.3 0.0 collective-permute-done.5
  47.3 1.7 %collective-permute-start.10 = (f32[1,2,2,3,8,256]{5,4,3,2,1,0:T(8,128)S(1)}, f32[1,2,2,3,8,256]{5,4,3,2,1,0:T(8,128)S(1)}, u32[]{:S(2)}, u32[]{:S(2)}) collective-permute-start(f32[1,2,2,3,8,256]{5,4,3,2,1,0:T(8,128)S(1)} %get-tuple-element.51), channel_id=1, source_target_pairs={{0,4},{4,0},{8,12},{12,8},{16,20},{20,16},{24,28},{28,24},{1,5},{5... | collective-permute-start | bytes 294920 | tf_op jit(solution)/shard_map/ppermute | solution.py:415
  49.0 4.0 %shard_map.72 = f32[4,2,2,3,8,256]{5,4,3,2,1,0:T(8,128)S(1)} custom-call(s32[8]{0:T(128)S(4)} %get-tuple-element.35.info_ref, bf16[512,5120]{1,0:T(8,128)(2,1)S(1)} %get-tuple-element.22.table_ref, bf16[3,16,5120]{2,1,0:T(8,128)(2,1)S(1)} %get-tuple-element.23.weight_ref), custom_call_target="tpu_custom_call" | custom-call | flops 6442450944 | bytes 4194304 | tf_op jit(solution)/shard_map/pallas_call | solution.py:270
  53.0 0.4 collective-permute-done.6
  53.4 0.1 slice_add_fusion.1
  53.5 1.7 %collective-permute-start.7 = (f32[2,2,2,3,8,256]{5,4,3,2,1,0:T(8,128)S(1)}, f32[2,2,2,3,8,256]{5,4,3,2,1,0:T(8,128)S(1)}, u32[]{:S(2)}, u32[]{:S(2)}) collective-permute-start(f32[2,2,2,3,8,256]{5,4,3,2,1,0:T(8,128)S(1)} %get-tuple-element.41), channel_id=1, source_target_pairs={{0,8},{4,12},{8,0},{12,4},{16,24},{20,28},{24,16},{28,20},{1,9},{5... | collective-permute-start | bytes 589832 | tf_op jit(solution)/shard_map/ppermute | solution.py:415
  55.1 0.0 collective-permute-done.3
  55.1 1.1 %collective-permute-start.8 = (f32[1,2,2,3,8,256]{5,4,3,2,1,0:T(8,128)S(1)}, f32[1,2,2,3,8,256]{5,4,3,2,1,0:T(8,128)S(1)}, u32[]{:S(2)}, u32[]{:S(2)}) collective-permute-start(f32[1,2,2,3,8,256]{5,4,3,2,1,0:T(8,128)S(1)} %get-tuple-element.54), channel_id=1, source_target_pairs={{0,16},{4,20},{8,24},{12,28},{16,0},{20,4},{24,8},{28,12},{1,17},{... | collective-permute-start | bytes 294920 | tf_op jit(solution)/shard_map/ppermute | solution.py:415
  56.2 3.1 %collective-permute-done.7 = f32[2,2,2,3,8,256]{5,4,3,2,1,0:T(8,128)S(1)} collective-permute-done((f32[2,2,2,3,8,256]{5,4,3,2,1,0:T(8,128)S(1)}, f32[2,2,2,3,8,256]{5,4,3,2,1,0:T(8,128)S(1)}, u32[]{:S(2)}, u32[]{:S(2)}) %collective-permute-start.7) | collective-permute-done | bytes 196640 | tf_op jit(solution)/shard_map/ppermute | solution.py:415
  59.3 3.1 %collective-permute-start.9 = (f32[1,2,2,3,8,256]{5,4,3,2,1,0:T(8,128)S(1)}, f32[1,2,2,3,8,256]{5,4,3,2,1,0:T(8,128)S(1)}, u32[]{:S(2)}, u32[]{:S(2)}) collective-permute-start(f32[1,2,2,3,8,256]{5,4,3,2,1,0:T(8,128)S(1)} %get-tuple-element.52), channel_id=1, source_target_pairs={{0,16},{4,20},{8,24},{12,28},{16,0},{20,4},{24,8},{28,12},{1,17},{... | collective-permute-start | bytes 294920 | tf_op jit(solution)/shard_map/ppermute | solution.py:415
  62.4 0.0 collective-permute-done.11.refs_3_
  62.4 0.0 collective-permute-done.10.refs_2_
  62.4 1.7 %shard_map.73 = (f32[2,64,256]{2,1,0:T(8,128)}, f32[32,128]{1,0:T(8,128)S(1)}) custom-call(f32[1,2,2,3,8,256]{5,4,3,2,1,0:T(8,128)S(1)} %get-tuple-element.50.refs_0_, f32[1,2,2,3,8,256]{5,4,3,2,1,0:T(8,128)S(1)} %get-tuple-element.48.refs_1_, f32[1,2,2,3,8,256]{5,4,3,2,1,0:T(8,128)S(1)} %collective-permute-done.10.refs_2_, ...), custom_call_target="tpu_custom_call" | custom-call | flops 1073741824 | bytes 1048576 | tf_op jit(solution)/shard_map/pallas_call | solution.py:364
  64.1 0.0 collective-permute-done.8.refs_2_
  64.1 0.9 %collective-permute-done.9.refs_3_ = f32[1,2,2,3,8,256]{5,4,3,2,1,0:T(8,128)S(1)} collective-permute-done((f32[1,2,2,3,8,256]{5,4,3,2,1,0:T(8,128)S(1)}, f32[1,2,2,3,8,256]{5,4,3,2,1,0:T(8,128)S(1)}, u32[]{:S(2)}, u32[]{:S(2)}) %collective-permute-start.9) | collective-permute-done | bytes 98336 | tf_op jit(solution)/shard_map/ppermute | solution.py:415
  65.0 1.7 %shard_map.74 = (f32[2,64,256]{2,1,0:T(8,128)}, f32[32,128]{1,0:T(8,128)S(1)}) custom-call(f32[1,2,2,3,8,256]{5,4,3,2,1,0:T(8,128)S(1)} %get-tuple-element.55.refs_0_, f32[1,2,2,3,8,256]{5,4,3,2,1,0:T(8,128)S(1)} %get-tuple-element.53.refs_1_, ...), custom_call_target="tpu_custom_call", output_to_operand_aliasing={{0}: (4, {}), {1}: (5, {})} | custom-call | flops 1073741824 | bytes 1048576 | tf_op jit(solution)/shard_map/pallas_call | solution.py:364
  66.7 13.1 %all_to_all.9 = f32[32,1,128]{2,1,0:T(1,128)S(1)} all-to-all(f32[32,1,128]{2,1,0:T(1,128)S(1)} %bitcast.7), channel_id=1, replica_groups=mesh['rows'=8,'feat'=4] {'rows','feat'}, dimensions={0} | all-to-all | bytes 32768 | tf_op jit(solution)/shard_map/all_to_all | solution.py:454
  79.8 0.6 reduce_max.9
  (4 shorter events, 0.1 us)
Async XLA Ops:
  12.2 22.3 %collective-permute-start = (f32[4,2,2,3,8,256]{5,4,3,2,1,0:T(8,128)S(1)}, f32[4,2,2,3,8,256]{5,4,3,2,1,0:T(8,128)S(1)}, u32[]{:S(2)}, u32[]{:S(2)}) collective-permute-start(f32[4,2,2,3,8,256]{5,4,3,2,1,0:T(8,128)S(1)} %get-tuple-element.30), channel_id=1, source_target_pairs={{0,8},{4,12},{8,0},{12,4},{16,24},{20,28},{24,16},{28,20},{1,9},{5... | collective-permute-start | bytes 1179656 | tf_op jit(solution)/shard_map/ppermute | solution.py:415
  22.3 12.1 %collective-permute-start.1 = (f32[4,2,2,3,8,256]{5,4,3,2,1,0:T(8,128)S(1)}, f32[4,2,2,3,8,256]{5,4,3,2,1,0:T(8,128)S(1)}, u32[]{:S(2)}, u32[]{:S(2)}) collective-permute-start(f32[4,2,2,3,8,256]{5,4,3,2,1,0:T(8,128)S(1)} %get-tuple-element.24), channel_id=1, source_target_pairs={{0,4},{4,0},{8,12},{12,8},{16,20},{20,16},{24,28},{28,24},{1,5},{5... | collective-permute-start | bytes 1179656 | tf_op jit(solution)/shard_map/ppermute | solution.py:415
  23.1 22.5 %collective-permute-start.2 = (f32[4,2,2,3,8,256]{5,4,3,2,1,0:T(8,128)S(1)}, f32[4,2,2,3,8,256]{5,4,3,2,1,0:T(8,128)S(1)}, u32[]{:S(2)}, u32[]{:S(2)}) collective-permute-start(f32[4,2,2,3,8,256]{5,4,3,2,1,0:T(8,128)S(1)} %get-tuple-element.25), channel_id=1, source_target_pairs={{0,4},{4,0},{8,12},{12,8},{16,20},{20,16},{24,28},{28,24},{1,5},{5... | collective-permute-start | bytes 1179656 | tf_op jit(solution)/shard_map/ppermute | solution.py:415
  34.4 12.2 %collective-permute-start.4 = (f32[2,2,2,3,8,256]{5,4,3,2,1,0:T(8,128)S(1)}, f32[2,2,2,3,8,256]{5,4,3,2,1,0:T(8,128)S(1)}, u32[]{:S(2)}, u32[]{:S(2)}) collective-permute-start(f32[2,2,2,3,8,256]{5,4,3,2,1,0:T(8,128)S(1)} %get-tuple-element.45), channel_id=1, source_target_pairs={{0,8},{4,12},{8,0},{12,4},{16,24},{20,28},{24,16},{28,20},{1,9},{5... | collective-permute-start | bytes 589832 | tf_op jit(solution)/shard_map/ppermute | solution.py:415
  34.6 12.7 %collective-permute-start.5 = (f32[2,2,2,3,8,256]{5,4,3,2,1,0:T(8,128)S(1)}, f32[2,2,2,3,8,256]{5,4,3,2,1,0:T(8,128)S(1)}, u32[]{:S(2)}, u32[]{:S(2)}) collective-permute-start(f32[2,2,2,3,8,256]{5,4,3,2,1,0:T(8,128)S(1)} %get-tuple-element.43), channel_id=1, source_target_pairs={{0,16},{4,20},{8,24},{12,28},{16,0},{20,4},{24,8},{28,12},{1,17},{... | collective-permute-start | bytes 589832 | tf_op jit(solution)/shard_map/ppermute | solution.py:415
  44.7 8.7 %collective-permute-start.6 = (f32[4,2,2,3,8,256]{5,4,3,2,1,0:T(8,128)S(1)}, f32[4,2,2,3,8,256]{5,4,3,2,1,0:T(8,128)S(1)}, u32[]{:S(2)}, u32[]{:S(2)}) collective-permute-start(f32[4,2,2,3,8,256]{5,4,3,2,1,0:T(8,128)S(1)} %get-tuple-element.33), channel_id=1, source_target_pairs={{0,4},{4,0},{8,12},{12,8},{16,20},{20,16},{24,28},{28,24},{1,5},{5... | collective-permute-start | bytes 1179656 | tf_op jit(solution)/shard_map/ppermute | solution.py:415
  45.7 9.4 %collective-permute-start.3 = (f32[2,2,2,3,8,256]{5,4,3,2,1,0:T(8,128)S(1)}, f32[2,2,2,3,8,256]{5,4,3,2,1,0:T(8,128)S(1)}, u32[]{:S(2)}, u32[]{:S(2)}) collective-permute-start(f32[2,2,2,3,8,256]{5,4,3,2,1,0:T(8,128)S(1)} %get-tuple-element.47), channel_id=1, source_target_pairs={{0,8},{4,12},{8,0},{12,4},{16,24},{20,28},{24,16},{28,20},{1,9},{5... | collective-permute-start | bytes 589832 | tf_op jit(solution)/shard_map/ppermute | solution.py:415
  46.7 15.8 %collective-permute-start.11 = (f32[1,2,2,3,8,256]{5,4,3,2,1,0:T(8,128)S(1)}, f32[1,2,2,3,8,256]{5,4,3,2,1,0:T(8,128)S(1)}, u32[]{:S(2)}, u32[]{:S(2)}) collective-permute-start(f32[1,2,2,3,8,256]{5,4,3,2,1,0:T(8,128)S(1)} %get-tuple-element.49), channel_id=1, source_target_pairs={{0,16},{4,20},{8,24},{12,28},{16,0},{20,4},{24,8},{28,12},{1,17},{... | collective-permute-start | bytes 294920 | tf_op jit(solution)/shard_map/ppermute | solution.py:415
  47.3 15.1 %collective-permute-start.10 = (f32[1,2,2,3,8,256]{5,4,3,2,1,0:T(8,128)S(1)}, f32[1,2,2,3,8,256]{5,4,3,2,1,0:T(8,128)S(1)}, u32[]{:S(2)}, u32[]{:S(2)}) collective-permute-start(f32[1,2,2,3,8,256]{5,4,3,2,1,0:T(8,128)S(1)} %get-tuple-element.51), channel_id=1, source_target_pairs={{0,4},{4,0},{8,12},{12,8},{16,20},{20,16},{24,28},{28,24},{1,5},{5... | collective-permute-start | bytes 294920 | tf_op jit(solution)/shard_map/ppermute | solution.py:415
  53.5 5.8 %collective-permute-start.7 = (f32[2,2,2,3,8,256]{5,4,3,2,1,0:T(8,128)S(1)}, f32[2,2,2,3,8,256]{5,4,3,2,1,0:T(8,128)S(1)}, u32[]{:S(2)}, u32[]{:S(2)}) collective-permute-start(f32[2,2,2,3,8,256]{5,4,3,2,1,0:T(8,128)S(1)} %get-tuple-element.41), channel_id=1, source_target_pairs={{0,8},{4,12},{8,0},{12,4},{16,24},{20,28},{24,16},{28,20},{1,9},{5... | collective-permute-start | bytes 589832 | tf_op jit(solution)/shard_map/ppermute | solution.py:415
  55.1 8.9 %collective-permute-start.8 = (f32[1,2,2,3,8,256]{5,4,3,2,1,0:T(8,128)S(1)}, f32[1,2,2,3,8,256]{5,4,3,2,1,0:T(8,128)S(1)}, u32[]{:S(2)}, u32[]{:S(2)}) collective-permute-start(f32[1,2,2,3,8,256]{5,4,3,2,1,0:T(8,128)S(1)} %get-tuple-element.54), channel_id=1, source_target_pairs={{0,16},{4,20},{8,24},{12,28},{16,0},{20,4},{24,8},{28,12},{1,17},{... | collective-permute-start | bytes 294920 | tf_op jit(solution)/shard_map/ppermute | solution.py:415
  59.3 5.7 %collective-permute-start.9 = (f32[1,2,2,3,8,256]{5,4,3,2,1,0:T(8,128)S(1)}, f32[1,2,2,3,8,256]{5,4,3,2,1,0:T(8,128)S(1)}, u32[]{:S(2)}, u32[]{:S(2)}) collective-permute-start(f32[1,2,2,3,8,256]{5,4,3,2,1,0:T(8,128)S(1)} %get-tuple-element.52), channel_id=1, source_target_pairs={{0,16},{4,20},{8,24},{12,28},{16,0},{20,4},{24,8},{28,12},{1,17},{... | collective-permute-start | bytes 294920 | tf_op jit(solution)/shard_map/ppermute | solution.py:415
